TPU v7x, 128 devices: a whole 4x4x4 slice. The times are simulated.
128 devices in a mesh: clus: 32 (over z, y, core), row: 4 (over x).
Axes of the slice: x: 4, y: 4, z: 4, core: 2. Of those that a mesh axis runs over, the one named last changes fastest.
Arguments:
- operator: bfloat16 [32, 1024, 32768], P(None, 'row', 'clus'), may hold values from -0.03125 to 0.03125
- omega: bfloat16 [32768, 256], P('clus'), may hold values from -6 to 6
- omega_rows: bfloat16 [32768, 256], P(('clus', 'row')), may hold values from -6 to 6
- near_list: int32 [32, 3], replicated, may hold values from 0 to 31, as said below
Outputs:
- col_basis: float32 [32768, 128], P(('clus', 'row'))
- row_basis: float32 [32768, 128], P(('clus', 'row'))
- col_transfers: float32 [32, 3, 256, 128], P('clus')
- row_transfers: float32 [32, 3, 256, 128], P('clus')
- col_top: float32 [32, 128, 256], P('clus')
- row_top: float32 [32, 128, 256], P('clus')
Inputs may be any that keep to these rules, and one draw needn't show every extreme that they name: `near_list`: row t lists 3 different clusters, the first being t itself.
All inputs are finite; a program needn't handle non-finite values.
Results may differ from a plain program's by a relative error of at most 0.0032.
Values may be sent and summed in bfloat16 or wider, within the bound.
A program may use at most 128 MiB of HBM per device.

v0:
```python
import math

import jax
import jax.numpy as jnp
from jax import lax
from jax.sharding import PartitionSpec as P

R = 128
MERGES = 3


HIGHEST = lax.Precision.HIGHEST


def partner(x, axis, apart):
    return lax.ppermute(x, axis, [(i, i ^ 1 << apart) for i in range(lax.axis_size(axis))])


def far_table(near_list, cluster_count):
    clusters = jnp.arange(cluster_count, dtype=jnp.int32)
    matched = near_list[:, :, None] == clusters[None, None, :]
    return 1.0 - jnp.max(matched.astype(jnp.float32), axis=1)


def local_gram(leading, stacked):
    return lax.dot_general(
        leading,
        stacked,
        (((0,), (0,)), ((), ())),
        precision=HIGHEST,
        preferred_element_type=jnp.float32,
    )


def finish(leading, gram_rows):
    factor_low = jnp.linalg.cholesky(gram_rows[:, :R])
    basis_part = lax.linalg.triangular_solve(
        factor_low, leading, left_side=False, lower=True, transpose_a=True
    )
    coeffs = lax.linalg.triangular_solve(factor_low, gram_rows, left_side=True, lower=True)
    return (basis_part, coeffs)


def factor_whole(stacked):
    leading = stacked[:, :R]
    return finish(leading, local_gram(leading, stacked))


def merge_step(own_part, sibling, on_left):
    left_first = jnp.concatenate([own_part, sibling], axis=0)
    right_first = jnp.concatenate([sibling, own_part], axis=0)
    return factor_whole(jnp.where(on_left, left_first, right_first))


def body(operator, omega, omega_rows, near_list):
    cluster_count = operator.shape[0]
    rows_share = operator.shape[1]
    width = operator.shape[2]
    my_index = lax.axis_index("clus")
    far = far_table(near_list, cluster_count)
    far_mine = lax.dynamic_index_in_dim(far, my_index, 1, keepdims=False)
    products = jnp.einsum("tij,js->tis", operator, omega, preferred_element_type=jnp.float32)
    products = (products * far_mine[:, None, None]).astype(jnp.bfloat16)
    received = lax.all_to_all(products, "clus", split_axis=0, concat_axis=0, tiled=True)
    operator_rows = operator.reshape(cluster_count * rows_share, width)
    block_part = lax.all_gather(omega_rows, "clus", axis=0, tiled=True)
    piece_rows = block_part.shape[0]
    owners = lax.iota(jnp.int32, piece_rows) // rows_share
    one_hot = (owners[:, None] == lax.iota(jnp.int32, cluster_count)[None, :]).astype(jnp.float32)
    weights = jnp.dot(one_hot, far_mine, precision=HIGHEST)
    scaled = block_part * weights.astype(jnp.bfloat16)[:, None]
    partial_sum = lax.dot_general(
        operator_rows, scaled, (((0,), (0,)), ((), ())), preferred_element_type=jnp.float32
    )
    sample_u = jnp.sum(received.astype(jnp.float32), axis=0)
    leading_u = sample_u[:, :R]
    gram_u_local = local_gram(leading_u, sample_u)
    share_v = lax.psum_scatter(partial_sum, "row", scatter_dimension=0, tiled=True)
    gram_v_local = local_gram(share_v[:, :R], share_v)
    gram_u, gram_v = lax.psum((gram_u_local, gram_v_local), "row")
    basis_u, coeffs_u = finish(leading_u, gram_u)
    basis_v, coeffs_v = finish(share_v[:, :R], gram_v)
    moved_u = []
    moved_v = []
    top_u, top_v = (coeffs_u, coeffs_v)
    for level_no in range(MERGES):
        sibling_u, sibling_v = partner((top_u, top_v), "clus", level_no)
        on_left = my_index >> level_no & 1 == 0
        trans_u, top_u = merge_step(top_u, sibling_u, on_left)
        trans_v, top_v = merge_step(top_v, sibling_v, on_left)
        moved_u.append(trans_u)
        moved_v.append(trans_v)
    scale = math.sqrt(width)
    pair_scale = math.sqrt(2 * R)
    col_transfers = jnp.stack(moved_u, axis=0)[None] * pair_scale
    row_transfers = jnp.stack(moved_v, axis=0)[None] * pair_scale
    return (
        basis_u * scale,
        basis_v * scale,
        col_transfers,
        row_transfers,
        (top_u / scale)[None],
        (top_v / scale)[None],
    )


def solution(mesh):
    in_specs = (P(None, "row", "clus"), P("clus", None), P(("clus", "row"), None), P())
    out_specs = (
        P(("clus", "row"), None),
        P(("clus", "row"), None),
        P("clus", None, None, None),
        P("clus", None, None, None),
        P("clus", None, None),
        P("clus", None, None),
    )
    return jax.shard_map(body, mesh=mesh, in_specs=in_specs, out_specs=out_specs, check_vma=False)
```

profile of v0, /device:TPU:1, one launch (start us, length us, event | category | flops | bytes accessed | tf_op | source)
XLA Modules:
  0.0 387.4 jit_solution(5616142430263085953)
XLA Ops:
  8.9 12.3 %multiply_convert_fusion = bf16[32,256,256]{2,1,0:T(8,128)(2,1)} fusion(f32[32]{0:T(128)S(1)} %fusion.78, bf16[32,256,1024]{2,1,0:T(8,128)(2,1)} %param.9, bf16[1024,256]{1,0:T(8,128)(2,1)S(1)} %copy-done), kind=kOutput, calls=%fused_computation.1 | convolution fusion | flops 4299161600 | bytes 21495936 | tf_op jit(solution)/shard_map/tij,js->tis/dot_general | solution.py:62
  21.2 9.7 %all-to-all-start = ((bf16[32,256,256]{2,1,0:T(8,128)(2,1)}), bf16[32,256,256]{2,1,0:T(8,128)(2,1)}, u32[]{:S(2)}, u32[]{:S(2)}) async-start(bf16[32,256,256]{2,1,0:T(8,128)(2,1)} %multiply_convert_fusion), calls=%async_computation | async-start | bytes 8388608 | tf_op jit(solution)/shard_map/all_to_all | solution.py:64
  31.3 57.4 %all-gather.2.cloned.1.call-done = bf16[8192,256]{1,0:T(8,128)(2,1)} async-done(((bf16[256,256]{1,0:T(8,128)(2,1)}), bf16[8192,256]{1,0:T(8,128)(2,1)}) %all-gather.2.cloned.1.call-update) | async-done | bytes 4194320 | tf_op jit(solution)/shard_map/all_gather | solution.py:66
  88.7 12.7 %fusion.3 = f32[1024,256]{0,1:T(8,128)} fusion(bf16[8192,1024]{1,0:T(8,128)(2,1)} %bitcast.168, bf16[8192,256]{1,0:T(8,128)(2,1)} %all-gather.2.cloned.1.call-done, bf16[8192]{0:T(1024)(128)(2,1)S(1)} %convert_element_type.16), kind=kOutput, calls=%fused_computation.5 | convolution fusion | flops 4297064448 | bytes 22036480 | tf_op jit(solution)/shard_map/dot_general | solution.py:72
  101.7 2.8 convert_reduce_fusion
  104.5 1.2 fusion.35
  105.7 19.0 %reduce-scatter.2.cloned.1.call-done = f32[256,256]{0,1:T(8,128)} async-done(((f32[1024,256]{0,1:T(8,128)}), f32[256,256]{0,1:T(8,128)}) %reduce-scatter.2.cloned.1.call-update) | async-done | bytes 262160 | tf_op jit(solution)/shard_map/reduce_scatter | solution.py:78
  124.7 2.1 fusion.32
  126.8 41.7 %all-reduce.3.cloned.1.call-done = (f32[128,256]{0,1:T(8,128)}, f32[128,256]{0,1:T(8,128)}) async-done(((f32[128,256]{0,1:T(8,128)}, f32[128,256]{0,1:T(8,128)}), (f32[128,256]{0,1:T(8,128)}, f32[128,256]{0,1:T(8,128)})) %all-reduce.3.cloned.1.call-update) | async-done | bytes 262160 | tf_op jit(solution)/shard_map/psum | solution.py:80
  170.4 11.7 %cholesky.145 = f32[128,128]{1,0:T(8,128)S(1)} custom-call(f32[128,128]{1,0:T(8,128)S(1)} %fusion.70), custom_call_target="Cholesky" | custom-call | tf_op jit(solution)/shard_map/jit(cholesky)/cholesky | solution.py:36
  183.4 9.8 %custom-call.23 = f32[1,128,128]{1,2,0:T(8,128)S(1)} custom-call(f32[1,128,128]{2,1,0:T(8,128)S(1)} %fusion.38), custom_call_target="InvertDiagBlocksLowerTriangular" | custom-call | tf_op jit(solution)/shard_map/triangular_solve/custom-call.0 | solution.py:37
  193.2 1.2 fusion.67
  194.4 3.1 collective-permute-start.3
  199.4 11.7 %cholesky.134 = f32[128,128]{1,0:T(8,128)S(1)} custom-call(f32[128,128]{1,0:T(8,128)S(1)} %fusion.74), custom_call_target="Cholesky" | custom-call | tf_op jit(solution)/shard_map/jit(cholesky)/cholesky | solution.py:36
  212.4 9.8 %custom-call.22 = f32[1,128,128]{1,2,0:T(8,128)S(1)} custom-call(f32[1,128,128]{2,1,0:T(8,128)S(1)} %fusion.37), custom_call_target="InvertDiagBlocksLowerTriangular" | custom-call | tf_op jit(solution)/shard_map/triangular_solve/custom-call.0 | solution.py:37
  222.2 1.2 fusion.71
  224.0 1.2 fusion.8
  227.7 11.7 %cholesky.189 = f32[128,128]{1,0:T(8,128)S(1)} custom-call(f32[128,128]{1,0:T(8,128)S(1)} %fusion.55), custom_call_target="Cholesky" | custom-call | tf_op jit(solution)/shard_map/jit(cholesky)/cholesky | solution.py:36
  240.7 9.8 %custom-call.31 = f32[1,128,128]{1,2,0:T(8,128)S(1)} custom-call(f32[1,128,128]{2,1,0:T(8,128)S(1)} %fusion.42), custom_call_target="InvertDiagBlocksLowerTriangular" | custom-call | tf_op jit(solution)/shard_map/triangular_solve/custom-call.0 | solution.py:37
  250.8 1.5 collective-permute-start.4
  252.8 11.7 %cholesky.156 = f32[128,128]{1,0:T(8,128)S(1)} custom-call(f32[128,128]{1,0:T(8,128)S(1)} %fusion.66), custom_call_target="Cholesky" | custom-call | tf_op jit(solution)/shard_map/jit(cholesky)/cholesky | solution.py:36
  265.9 9.8 %custom-call.25 = f32[1,128,128]{1,2,0:T(8,128)S(1)} custom-call(f32[1,128,128]{2,1,0:T(8,128)S(1)} %fusion.39), custom_call_target="InvertDiagBlocksLowerTriangular" | custom-call | tf_op jit(solution)/shard_map/triangular_solve/custom-call.0 | solution.py:37
  277.8 11.7 %cholesky.200 = f32[128,128]{1,0:T(8,128)S(1)} custom-call(f32[128,128]{1,0:T(8,128)S(1)} %fusion.51), custom_call_target="Cholesky" | custom-call | tf_op jit(solution)/shard_map/jit(cholesky)/cholesky | solution.py:36
  290.8 9.8 %custom-call.33 = f32[1,128,128]{1,2,0:T(8,128)S(1)} custom-call(f32[1,128,128]{2,1,0:T(8,128)S(1)} %fusion.43), custom_call_target="InvertDiagBlocksLowerTriangular" | custom-call | tf_op jit(solution)/shard_map/triangular_solve/custom-call.0 | solution.py:37
  301.0 3.1 collective-permute-start.5
  304.6 11.7 %cholesky.167 = f32[128,128]{1,0:T(8,128)S(1)} custom-call(f32[128,128]{1,0:T(8,128)S(1)} %fusion.62), custom_call_target="Cholesky" | custom-call | tf_op jit(solution)/shard_map/jit(cholesky)/cholesky | solution.py:36
  317.6 9.8 %custom-call.27 = f32[1,128,128]{1,2,0:T(8,128)S(1)} custom-call(f32[1,128,128]{2,1,0:T(8,128)S(1)} %fusion.40), custom_call_target="InvertDiagBlocksLowerTriangular" | custom-call | tf_op jit(solution)/shard_map/triangular_solve/custom-call.0 | solution.py:37
  329.6 11.7 %cholesky.211 = f32[128,128]{1,0:T(8,128)S(1)} custom-call(f32[128,128]{1,0:T(8,128)S(1)} %fusion.47), custom_call_target="Cholesky" | custom-call | tf_op jit(solution)/shard_map/jit(cholesky)/cholesky | solution.py:36
  342.6 9.8 %custom-call.35 = f32[1,128,128]{1,2,0:T(8,128)S(1)} custom-call(f32[1,128,128]{2,1,0:T(8,128)S(1)} %fusion.44), custom_call_target="InvertDiagBlocksLowerTriangular" | custom-call | tf_op jit(solution)/shard_map/triangular_solve/custom-call.0 | solution.py:37
  354.3 11.7 %cholesky.178 = f32[128,128]{1,0:T(8,128)S(1)} custom-call(f32[128,128]{1,0:T(8,128)S(1)} %fusion.58), custom_call_target="Cholesky" | custom-call | tf_op jit(solution)/shard_map/jit(cholesky)/cholesky | solution.py:36
  367.3 9.8 %custom-call.29 = f32[1,128,128]{1,2,0:T(8,128)S(1)} custom-call(f32[1,128,128]{2,1,0:T(8,128)S(1)} %fusion.41), custom_call_target="InvertDiagBlocksLowerTriangular" | custom-call | tf_op jit(solution)/shard_map/triangular_solve/custom-call.0 | solution.py:37
  377.2 1.0 fusion.7
  (100 shorter events, 29.3 us)
Async XLA Ops:
  7.2 1.7 copy-start
  7.2 81.5 %all-gather.2.cloned.1.call-start = ((), (), s32[]{:S(2)}) async-start(), calls=%async_computation.2 | async-start | bytes 4325376 | tf_op jit(solution)/shard_map/all_gather | solution.py:66
  21.2 80.5 %all-to-all-start = ((bf16[32,256,256]{2,1,0:T(8,128)(2,1)}), bf16[32,256,256]{2,1,0:T(8,128)(2,1)}, u32[]{:S(2)}, u32[]{:S(2)}) async-start(bf16[32,256,256]{2,1,0:T(8,128)(2,1)} %multiply_convert_fusion), calls=%async_computation | async-start | bytes 8388608 | tf_op jit(solution)/shard_map/all_to_all | solution.py:64
  30.8 93.9 %reduce-scatter.2.cloned.1.call-start = ((), (), s32[]{:S(2)}) async-start(), calls=%async_computation.3 | async-start | bytes 1310720 | tf_op jit(solution)/shard_map/reduce_scatter | solution.py:78
  101.4 67.1 %all-reduce.3.cloned.1.call-start = ((), (), s32[]{:S(2)}) async-start(), calls=%async_computation.4 | async-start | bytes 524288 | tf_op jit(solution)/shard_map/psum | solution.py:80
  194.4 32.6 %collective-permute-start.3 = (f32[128,256]{1,0:T(8,128)S(1)}, f32[128,256]{1,0:T(8,128)S(1)}, u32[]{:S(2)}, u32[]{:S(2)}) collective-permute-start(f32[128,256]{1,0:T(8,128)S(1)} %fusion.67), channel_id=1, source_target_pairs={{0,4},{4,0},{8,12},{12,8},{16,20},{20,16},{24,28},{28,24},{32,36},... | collective-permute-start | bytes 393224 | tf_op jit(solution)/shard_map/ppermute | solution.py:16
  223.5 3.6 collective-permute-start
  250.8 26.4 %collective-permute-start.4 = (f32[128,256]{1,0:T(8,128)S(1)}, f32[128,256]{1,0:T(8,128)S(1)}, u32[]{:S(2)}, u32[]{:S(2)}) collective-permute-start(f32[128,256]{1,0:T(8,128)S(1)} %fusion.52), channel_id=1, source_target_pairs={{0,8},{4,12},{8,0},{12,4},{16,24},{20,28},{24,16},{28,20},{32,40},... | collective-permute-start | bytes 393224 | tf_op jit(solution)/shard_map/ppermute | solution.py:16
  276.3 27.7 %collective-permute-start.1 = (f32[128,256]{1,0:T(8,128)S(1)}, f32[128,256]{1,0:T(8,128)S(1)}, u32[]{:S(2)}, u32[]{:S(2)}) collective-permute-start(f32[128,256]{1,0:T(8,128)S(1)} %fusion.63), channel_id=1, source_target_pairs={{0,8},{4,12},{8,0},{12,4},{16,24},{20,28},{24,16},{28,20},{32,40},... | collective-permute-start | bytes 393224 | tf_op jit(solution)/shard_map/ppermute | solution.py:16
  301.0 28.1 %collective-permute-start.5 = (f32[128,256]{1,0:T(8,128)S(1)}, f32[128,256]{1,0:T(8,128)S(1)}, u32[]{:S(2)}, u32[]{:S(2)}) collective-permute-start(f32[128,256]{1,0:T(8,128)S(1)} %fusion.48), channel_id=1, source_target_pairs={{0,16},{4,20},{8,24},{12,28},{16,0},{20,4},{24,8},{28,12},{32,48},... | collective-permute-start | bytes 393224 | tf_op jit(solution)/shard_map/ppermute | solution.py:16
  328.1 25.7 %collective-permute-start.2 = (f32[128,256]{1,0:T(8,128)S(1)}, f32[128,256]{1,0:T(8,128)S(1)}, u32[]{:S(2)}, u32[]{:S(2)}) collective-permute-start(f32[128,256]{1,0:T(8,128)S(1)} %fusion.59), channel_id=1, source_target_pairs={{0,16},{4,20},{8,24},{12,28},{16,0},{20,4},{24,8},{28,12},{32,48},... | collective-permute-start | bytes 393224 | tf_op jit(solution)/shard_map/ppermute | solution.py:16
Sparse Core Ops, SparseCore 0:
  10.3 78.3 all-gather.1
  101.5 23.1 reduce-scatter.1
  127.8 40.6 all-reduce.2
where the time goes:
time: 395 us; the launch traced here: 387 us
  other arithmetic  189 us (48%)
  waiting for transfers between devices  119 us (30%)
  matrix products  40 us (10%)
  starting transfers between devices  19.4 us (5%)
  between operations  14.9 us (4%)
  local copies, waits for them, and re-layouts  5.78 us (1%)
    another operation x24, other arithmetic, finish(): factor_low = jnp.linalg.cholesky(gram_rows[:, :R])  99.1 us
    another operation x16, other arithmetic, finish(): lax.linalg.triangular_solve(factor_low, leading, left_side=False, lower=T...  83.7 us
    all_gather x1, waiting for transfers between devices, body(): block_part = lax.all_gather(omega_rows, 'clus', axis=0, tiled=True)  57.4 us
    psum x1, waiting for transfers between devices, body(): gram_u, gram_v = lax.psum((gram_u_local, gram_v_local), 'row')  41.7 us
    reduce_scatter x1, waiting for transfers between devices, body(): lax.psum_scatter(partial_sum, 'row', scatter_dimension=0, tiled=True)  19 us
    dot_general x1, matrix products, body(): lax.dot_general(operator_rows, scaled, (((0,), (0,)), ((), ())), preferre...  12.7 us
    dot_general x1, matrix products, body(): jnp.einsum('tij,js->tis', operator, omega, preferred_element_type=jnp.flo...  12.3 us
    all_to_all x1, starting transfers between devices, body(): lax.all_to_all(products, 'clus', split_axis=0, concat_axis=0, tiled=True)  9.66 us
  transfers between devices with their start and end apart: 10, of which 3 were waited for; matrix products, arithmetic and copies ran while one was open for 40% of the time, Pallas kernels for 0%

commit v1 on v0

--- a/solution.py
+++ b/solution.py
@@ -3,9 +3,12 @@
 import jax
 import jax.numpy as jnp
 from jax import lax
+from jax.experimental import pallas as pl
+from jax.experimental.pallas import tpu as pltpu
 from jax.sharding import PartitionSpec as P
 
 R = 128
+F32 = jnp.float32
 MERGES = 3
 
 
@@ -32,24 +35,91 @@
     )
 
 
-def finish(leading, gram_rows):
-    factor_low = jnp.linalg.cholesky(gram_rows[:, :R])
-    basis_part = lax.linalg.triangular_solve(
-        factor_low, leading, left_side=False, lower=True, transpose_a=True
-    )
-    coeffs = lax.linalg.triangular_solve(factor_low, gram_rows, left_side=True, lower=True)
-    return (basis_part, coeffs)
+def split3(x):
+    hi = x.astype(jnp.bfloat16).astype(F32)
+    rest = x - hi
+    mid = rest.astype(jnp.bfloat16).astype(F32)
+    low = rest - mid
+    return hi, mid, low
+
+def panel(state, m, first):
+    rows = state[m, first:first + 8, :]
+    place = lax.broadcasted_iota(jnp.int32, (8, R), 0)
+    place2 = lax.broadcasted_iota(jnp.int32, (8, 2 * R), 0)
+    cols = [jnp.broadcast_to(rows[:, first + c:first + c + 1], (8, R)) for c in range(8)]
+    for c in range(8):
+        scale = lax.rsqrt(jnp.broadcast_to(cols[c][c:c + 1, :], (8, R)))
+        mult = jnp.where(place > c, cols[c] * scale, 0.0)
+        for k in range(c + 1, 8):
+            cols[k] = cols[k] - mult * (jnp.broadcast_to(cols[k][c:c + 1, :], (8, R)) * scale)
+        scale2 = jnp.concatenate([scale, scale], axis=1)
+        mult2 = jnp.concatenate([mult, mult], axis=1)
+        pivot = jnp.broadcast_to(rows[c:c + 1, :], (8, 2 * R)) * scale2
+        rows = jnp.where(place2 == c, pivot, rows - mult2 * pivot)
+    state[m, first:first + 8, :] = rows
+    last = first + 8
+    if last < R:
+        hi, mid, low = split3(rows)
+        left = jnp.concatenate([hi, hi, mid, mid, hi, low], axis=0).astype(jnp.bfloat16)
+        right = jnp.concatenate([hi, mid, hi, mid, low, hi], axis=0).astype(jnp.bfloat16)
+        state[m, last:, :] -= lax.dot_general(left[:, last:R] if last % R == 0 else left[:, :R], right, (((0,), (0,)), ((), ())), preferred_element_type=F32)[last:, :]
+
+def chol_all(state, count):
+    for first in range(0, R, 8):
+        for m in range(count):
+            panel(state, m, first)
+
+def factor_kernel(bits_ref, gram_ref, side_ref, sample_ref, basis_ref, trans_ref, top_ref, state):
+    eye_rows = lax.broadcasted_iota(jnp.int32, (R, R), 0)
+    eye_cols = lax.broadcasted_iota(jnp.int32, (R, R), 1)
+    eye = (eye_rows == eye_cols).astype(F32)
+    count = gram_ref.shape[0]
+    for m in range(count):
+        state[m, :, :R] = gram_ref[m]
+        state[m, :, R:] = eye
+    chol_all(state, count)
+    for m in range(count):
+        state[m, :, :R] = jnp.where(eye_cols >= eye_rows, state[m, :, :R], 0.0)
+    half = count // 2
+    outer = (((1,), (1,)), ((), ()))
+    for s in range(2):
+        inverse = state[s * half + bits_ref[0], :, R:]
+        basis_ref[s] = lax.dot_general(
+            sample_ref[s], inverse, outer, precision=HIGHEST, preferred_element_type=F32
+        ) * math.sqrt(1024)
+        for k in range(MERGES):
+            at = 2 * (k + 1) + (bits_ref[k + 1] if k + 1 < MERGES else 0)
+            inverse = state[s * half + at, :, R:] * math.sqrt(2 * R)
+            for h in range(2):
+                trans_ref[s, k, h * R:(h + 1) * R, :] = lax.dot_general(
+                    state[s * half + 2 * k + h, :, :R],
+                    inverse,
+                    outer,
+                    precision=HIGHEST,
+                    preferred_element_type=F32,
+                )
+        last = s * half + 2 * MERGES
+        top_ref[s, :, :R] = state[last, :, :R] * (1.0 / math.sqrt(1024))
+        top_ref[s, :, R:] = jnp.dot(
+            state[last, :, R:], side_ref[s], precision=HIGHEST, preferred_element_type=F32
+        ) * (1.0 / math.sqrt(1024))
 
 
-def factor_whole(stacked):
-    leading = stacked[:, :R]
-    return finish(leading, local_gram(leading, stacked))
-
-
-def merge_step(own_part, sibling, on_left):
-    left_first = jnp.concatenate([own_part, sibling], axis=0)
-    right_first = jnp.concatenate([sibling, own_part], axis=0)
-    return factor_whole(jnp.where(on_left, left_first, right_first))
+def factor_all(bits, grams, side, samples):
+    vmem = pl.BlockSpec(memory_space=pltpu.VMEM)
+    count, rows = grams.shape[0], samples.shape[1]
+    return pl.pallas_call(
+        factor_kernel,
+        out_shape=[
+            jax.ShapeDtypeStruct((2, rows, R), F32),
+            jax.ShapeDtypeStruct((2, MERGES, 2 * R, R), F32),
+            jax.ShapeDtypeStruct((2, R, 2 * R), F32),
+        ],
+        in_specs=[pl.BlockSpec(memory_space=pltpu.SMEM), vmem, vmem, vmem],
+        out_specs=[vmem, vmem, vmem],
+        scratch_shapes=[pltpu.VMEM((count, R, 2 * R), F32)],
+        compiler_params=pltpu.CompilerParams(vmem_limit_bytes=40 << 20),
+    )(bits, grams, side, samples)
 
 
 def body(operator, omega, omega_rows, near_list):
@@ -78,30 +148,20 @@
     share_v = lax.psum_scatter(partial_sum, "row", scatter_dimension=0, tiled=True)
     gram_v_local = local_gram(share_v[:, :R], share_v)
     gram_u, gram_v = lax.psum((gram_u_local, gram_v_local), "row")
-    basis_u, coeffs_u = finish(leading_u, gram_u)
-    basis_v, coeffs_v = finish(share_v[:, :R], gram_v)
-    moved_u = []
-    moved_v = []
-    top_u, top_v = (coeffs_u, coeffs_v)
+    total = jnp.stack([gram_u, gram_v])
+    ordered = []
     for level_no in range(MERGES):
-        sibling_u, sibling_v = partner((top_u, top_v), "clus", level_no)
+        sibling = partner(total, "clus", level_no)
         on_left = my_index >> level_no & 1 == 0
-        trans_u, top_u = merge_step(top_u, sibling_u, on_left)
-        trans_v, top_v = merge_step(top_v, sibling_v, on_left)
-        moved_u.append(trans_u)
-        moved_v.append(trans_v)
-    scale = math.sqrt(width)
-    pair_scale = math.sqrt(2 * R)
-    col_transfers = jnp.stack(moved_u, axis=0)[None] * pair_scale
-    row_transfers = jnp.stack(moved_v, axis=0)[None] * pair_scale
-    return (
-        basis_u * scale,
-        basis_v * scale,
-        col_transfers,
-        row_transfers,
-        (top_u / scale)[None],
-        (top_v / scale)[None],
-    )
+        ordered.append(jnp.where(on_left, total, sibling)[:, :, :R])
+        ordered.append(jnp.where(on_left, sibling, total)[:, :, :R])
+        total = total + sibling
+    ordered.append(total[:, :, :R])
+    grams = jnp.stack(ordered, axis=1).reshape(2 * (2 * MERGES + 1), R, R)
+    bits = (my_index >> jnp.arange(4, dtype=jnp.int32)) & 1
+    samples = jnp.stack([leading_u, share_v[:, :R]])
+    basis, trans, top = factor_all(bits, grams, total[:, :, R:], samples)
+    return (basis[0], basis[1], trans[0][None], trans[1][None], top[0][None], top[1][None])
 
 
 def solution(mesh):

time: 395 us -> 218 us (0.55); the launches traced: 387 us -> 216 us
  other arithmetic: 189 us -> 4 us
  Pallas kernels: 0 us -> 16.7 us
  waiting for transfers between devices: 119 us -> 131 us
  matrix products: 40 us -> 28.7 us
    another operation x40 -> x1, other arithmetic: 183 us -> 0.02 us  [body(): samples = jnp.stack([leading_u, share_v[:, :R]])]
    pallas_call x0 -> x1, Pallas kernels: none -> 16.7 us  [factor_all(): pl.pallas_call(factor_kernel, out_shape=[jax.ShapeDtypeStruct((2, rows, R...]
    ppermute x6 -> x3, waiting for transfers between devices: 0.02 us -> 11.8 us  [partner(): lax.ppermute(x, axis, [(i, i ^ 1 << apart) for i in range(lax.axis_size(a...]
    another operation x16 -> x0, matrix products: 8.98 us -> none  [the longest x8 5.61 us: finish(): lax.linalg.triangular_solve(factor_low, gram_rows, left_side=True, lower=...]
    ppermute x6 -> x3, starting transfers between devices: 9.37 us -> 7.15 us  [partner(): lax.ppermute(x, axis, [(i, i ^ 1 << apart) for i in range(lax.axis_size(a...]
  transfers between devices with their start and end apart: 10 -> 7, of which waited for: 3 -> 6; matrix products, arithmetic and copies ran while one was open for 40% -> 15% of each run, Pallas kernels for 0% -> 0%
where the time goes in v1:
time: 218 us; the launch traced here: 216 us
  waiting for transfers between devices  131 us (60%)
  matrix products  28.7 us (13%)
  starting transfers between devices  16.9 us (8%)
  Pallas kernels  16.7 us (8%)
  between operations  13.9 us (6%)
  local copies, waits for them, and re-layouts  5.2 us (2%)
  other arithmetic  4 us (2%)
    all_gather x1, waiting for transfers between devices, body(): block_part = lax.all_gather(omega_rows, 'clus', axis=0, tiled=True)  57.4 us
    psum x1, waiting for transfers between devices, body(): gram_u, gram_v = lax.psum((gram_u_local, gram_v_local), 'row')  41.7 us
    reduce_scatter x1, waiting for transfers between devices, body(): lax.psum_scatter(partial_sum, 'row', scatter_dimension=0, tiled=True)  19.3 us
    pallas_call x1, Pallas kernels, factor_all(): pl.pallas_call(factor_kernel, out_shape=[jax.ShapeDtypeStruct((2, rows, R...  16.7 us
    dot_general x1, matrix products, body(): lax.dot_general(operator_rows, scaled, (((0,), (0,)), ((), ())), preferre...  12.9 us
    dot_general x1, matrix products, body(): jnp.einsum('tij,js->tis', operator, omega, preferred_element_type=jnp.flo...  12.3 us
    ppermute x3, waiting for transfers between devices, partner(): lax.ppermute(x, axis, [(i, i ^ 1 << apart) for i in range(lax.axis_size(a...  11.8 us
    all_to_all x1, starting transfers between devices, body(): lax.all_to_all(products, 'clus', split_axis=0, concat_axis=0, tiled=True)  9.66 us
  transfers between devices with their start and end apart: 7, of which 6 were waited for; matrix products, arithmetic and copies ran while one was open for 15% of the time, Pallas kernels for 0%

profile of v1, /device:TPU:1, one launch (start us, length us, event | category | flops | bytes accessed | tf_op | source)
XLA Modules:
  0.0 216.5 jit_solution(16071528886855512470)
XLA Ops:
  7.2 0.0 all-gather.2.cloned.1.call-start
  7.2 0.7 all-gather.2.cloned.1.call-update
  7.9 0.8 convert_reduce_fusion.1
  8.7 0.2 fusion.15
  8.9 12.3 %multiply_convert_fusion = bf16[32,256,256]{2,1,0:T(8,128)(2,1)} fusion(f32[32]{0:T(128)S(1)} %fusion.15, bf16[32,256,1024]{2,1,0:T(8,128)(2,1)} %param.4, bf16[1024,256]{1,0:T(8,128)(2,1)S(1)} %copy-done), kind=kOutput, calls=%fused_computation.1 | convolution fusion | flops 4299161600 | bytes 21495936 | tf_op jit(solution)/shard_map/tij,js->tis/dot_general | solution.py:132
  21.2 9.7 %all-to-all-start = ((bf16[32,256,256]{2,1,0:T(8,128)(2,1)}), bf16[32,256,256]{2,1,0:T(8,128)(2,1)}, u32[]{:S(2)}, u32[]{:S(2)}) async-start(bf16[32,256,256]{2,1,0:T(8,128)(2,1)} %multiply_convert_fusion), calls=%async_computation | async-start | bytes 8388608 | tf_op jit(solution)/shard_map/all_to_all | solution.py:134
  30.8 0.0 reduce-scatter.2.cloned.1.call-start
  30.9 0.4 fusion.6
  31.3 57.4 %all-gather.2.cloned.1.call-done = bf16[8192,256]{1,0:T(8,128)(2,1)} async-done(((bf16[256,256]{1,0:T(8,128)(2,1)}), bf16[8192,256]{1,0:T(8,128)(2,1)}) %all-gather.2.cloned.1.call-update) | async-done | bytes 4194320 | tf_op jit(solution)/shard_map/all_gather | solution.py:136
  88.7 12.9 %fusion.3 = f32[1024,256]{1,0:T(8,128)} fusion(bf16[8192,1024]{1,0:T(8,128)(2,1)} %bitcast.45, bf16[8192,256]{1,0:T(8,128)(2,1)} %all-gather.2.cloned.1.call-done, bf16[8192]{0:T(1024)(128)(2,1)S(1)} %convert_element_type.16), kind=kOutput, calls=%fused_computation.5 | convolution fusion | flops 4297064448 | bytes 22036480 | tf_op jit(solution)/shard_map/dot_general | solution.py:142
  101.6 0.0 reduce-scatter.2.cloned.1.call-update
  101.7 0.0 all-reduce.3.cloned.1.call-start
  101.7 2.8 %convert_reduce_fusion = f32[256,256]{1,0:T(8,128)S(1)} fusion(bf16[32,256,256]{2,1,0:T(8,128)(2,1)} %all-to-all-done), kind=kLoop, calls=%fused_computation | loop fusion | flops 4128768 | bytes 4456448 | tf_op jit(solution)/shard_map/reduce_sum | solution.py:145
  104.5 1.1 convolution_bitcast_fusion.1
  105.6 19.3 %reduce-scatter.2.cloned.1.call-done = f32[256,256]{1,0:T(8,128)} async-done(((f32[1024,256]{1,0:T(8,128)}), f32[256,256]{1,0:T(8,128)}) %reduce-scatter.2.cloned.1.call-update) | async-done | bytes 262160 | tf_op jit(solution)/shard_map/reduce_scatter | solution.py:148
  124.9 2.1 convolution_bitcast_fusion
  127.0 0.0 all-reduce.3.cloned.1.call-update
  127.1 41.7 %all-reduce.3.cloned.1.call-done = (f32[1,128,256]{2,1,0:T(8,128)}, f32[1,128,256]{2,1,0:T(8,128)}) async-done(((f32[1,128,256]{2,1,0:T(8,128)}, f32[1,128,256]{2,1,0:T(8,128)}), (f32[1,128,256]{2,1,0:T(8,128)}, f32[1,128,256]{2,1,0:T(8,128)})) %all-reduce.3.cloned.1.call-update) | async-done | bytes 262160 | tf_op jit(solution)/shard_map/psum | solution.py:150
  168.8 0.9 constant_dynamic-update-slice_fusion.1
  169.7 0.9 constant_dynamic-update-slice_fusion
  170.6 2.9 %collective-permute-start = (f32[2,128,256]{2,1,0:T(8,128)S(1)}, f32[2,128,256]{2,1,0:T(8,128)S(1)}, u32[]{:S(2)}, u32[]{:S(2)}) collective-permute-start(f32[2,128,256]{2,1,0:T(8,128)S(1)} %constant_dynamic-update-slice_fusion), channel_id=1, source_target_pairs={{0,4},{4,0},{8,12},{12,8},{16,20},{20,16},{24,28},{28,24},{32,36},... | collective-permute-start | bytes 786440 | tf_op jit(solution)/shard_map/ppermute | solution.py:19
  173.5 0.9 slice_bitcast_fusion.3
  174.4 0.2 collective-permute-done
  174.7 1.3 collective-permute-start.1
  176.0 6.3 %collective-permute-done.1 = f32[2,128,256]{2,1,0:T(8,128)S(1)} collective-permute-done((f32[2,128,256]{2,1,0:T(8,128)S(1)}, f32[2,128,256]{2,1,0:T(8,128)S(1)}, u32[]{:S(2)}, u32[]{:S(2)}) %collective-permute-start.1) | collective-permute-done | bytes 262176 | tf_op jit(solution)/shard_map/ppermute | solution.py:19
  182.3 3.0 %collective-permute-start.2 = (f32[2,128,256]{2,1,0:T(8,128)S(1)}, f32[2,128,256]{2,1,0:T(8,128)S(1)}, u32[]{:S(2)}, u32[]{:S(2)}) collective-permute-start(f32[2,128,256]{2,1,0:T(8,128)S(1)} %add.26), channel_id=1, source_target_pairs={{0,16},{4,20},{8,24},{12,28},{16,0},{20,4},{24,8},{28,12},{32,48},... | collective-permute-start | bytes 786440 | tf_op jit(solution)/shard_map/ppermute | solution.py:19
  185.4 5.3 %collective-permute-done.2 = f32[2,128,256]{2,1,0:T(8,128)S(1)} collective-permute-done((f32[2,128,256]{2,1,0:T(8,128)S(1)}, f32[2,128,256]{2,1,0:T(8,128)S(1)}, u32[]{:S(2)}, u32[]{:S(2)}) %collective-permute-start.2) | collective-permute-done | bytes 262176 | tf_op jit(solution)/shard_map/ppermute | solution.py:19
  190.8 0.1 copy.18
  190.9 16.7 %shard_map.91 = (f32[2,256,128]{2,1,0:T(8,128)S(1)}, f32[2,3,256,128]{3,2,1,0:T(8,128)S(1)}, f32[2,128,256]{2,1,0:T(8,128)S(1)}) custom-call(s32[4]{0:T(128)S(1)} %shift-right-arithmetic_and_fusion.bits_ref, f32[14,128,128]{2,1,0:T(8,128)S(1)} %bitcast.43, f32[2,128,128]{2,1,0:T(8,128)S(1)} %slice.80.side_ref, f32[2,256,128]{2,1,0:T(8,128)S(1)} %pad_maximum_fusion.sample_ref), custom_call_target="tpu_custom_call" | custom-call | tf_op jit(solution)/shard_map/pallas_call | solution.py:111
  207.6 0.9 fusion.17
  208.5 0.7 fusion.18
  209.2 0.7 slice_bitcast_fusion.1
  (19 shorter events, 0.3 us)
Async XLA Ops:
  7.2 1.7 copy-start
  7.2 81.6 %all-gather.2.cloned.1.call-start = ((), (), s32[]{:S(2)}) async-start(), calls=%async_computation.2 | async-start | bytes 4325376 | tf_op jit(solution)/shard_map/all_gather | solution.py:136
  21.2 80.6 %all-to-all-start = ((bf16[32,256,256]{2,1,0:T(8,128)(2,1)}), bf16[32,256,256]{2,1,0:T(8,128)(2,1)}, u32[]{:S(2)}, u32[]{:S(2)}) async-start(bf16[32,256,256]{2,1,0:T(8,128)(2,1)} %multiply_convert_fusion), calls=%async_computation | async-start | bytes 8388608 | tf_op jit(solution)/shard_map/all_to_all | solution.py:134
  30.8 94.1 %reduce-scatter.2.cloned.1.call-start = ((), (), s32[]{:S(2)}) async-start(), calls=%async_computation.3 | async-start | bytes 1310720 | tf_op jit(solution)/shard_map/reduce_scatter | solution.py:148
  101.7 67.1 %all-reduce.3.cloned.1.call-start = ((), (), s32[]{:S(2)}) async-start(), calls=%async_computation.4 | async-start | bytes 524288 | tf_op jit(solution)/shard_map/psum | solution.py:150
  170.6 4.0 %collective-permute-start = (f32[2,128,256]{2,1,0:T(8,128)S(1)}, f32[2,128,256]{2,1,0:T(8,128)S(1)}, u32[]{:S(2)}, u32[]{:S(2)}) collective-permute-start(f32[2,128,256]{2,1,0:T(8,128)S(1)} %constant_dynamic-update-slice_fusion), channel_id=1, source_target_pairs={{0,4},{4,0},{8,12},{12,8},{16,20},{20,16},{24,28},{28,24},{32,36},... | collective-permute-start | bytes 786440 | tf_op jit(solution)/shard_map/ppermute | solution.py:19
  174.7 7.6 %collective-permute-start.1 = (f32[2,128,256]{2,1,0:T(8,128)S(1)}, f32[2,128,256]{2,1,0:T(8,128)S(1)}, u32[]{:S(2)}, u32[]{:S(2)}) collective-permute-start(f32[2,128,256]{2,1,0:T(8,128)S(1)} %add.25), channel_id=1, source_target_pairs={{0,8},{4,12},{8,0},{12,4},{16,24},{20,28},{24,16},{28,20},{32,40},... | collective-permute-start | bytes 786440 | tf_op jit(solution)/shard_map/ppermute | solution.py:19
  182.3 8.4 %collective-permute-start.2 = (f32[2,128,256]{2,1,0:T(8,128)S(1)}, f32[2,128,256]{2,1,0:T(8,128)S(1)}, u32[]{:S(2)}, u32[]{:S(2)}) collective-permute-start(f32[2,128,256]{2,1,0:T(8,128)S(1)} %add.26), channel_id=1, source_target_pairs={{0,16},{4,20},{8,24},{12,28},{16,0},{20,4},{24,8},{28,12},{32,48},... | collective-permute-start | bytes 786440 | tf_op jit(solution)/shard_map/ppermute | solution.py:19
Sparse Core Ops, SparseCore 0:
  10.3 78.4 all-gather.1
  101.8 23.0 reduce-scatter.1
  128.0 40.7 all-reduce.2

commit v2 on v1

--- a/solution.py
+++ b/solution.py
@@ -122,30 +122,317 @@
     )(bits, grams, side, samples)
 
 
+SIDE = 4
+MESH = pl.DeviceIdType.MESH
+
+
+def place_of():
+    clus = lax.axis_index("clus")
+    return (clus // 8, clus // 2 % SIDE, clus % 2)
+
+
+def clus_at(z, y, core):
+    return {"clus": (z % SIDE * SIDE + y % SIDE) * 2 + core}
+
+
+def remote(src, dst, send, recv, device):
+    return pltpu.make_async_remote_copy(
+        src_ref=src, dst_ref=dst, send_sem=send, recv_sem=recv, device_id=device, device_id_type=MESH
+    )
+
+
+def meet(devices):
+    barrier = pltpu.get_barrier_semaphore()
+    for device in devices:
+        pl.semaphore_signal(barrier, inc=1, device_id=device, device_id_type=MESH)
+    pl.semaphore_wait(barrier, len(devices))
+
+
+def sample_kernel(
+    far, op_hbm, omega, q_own, u_out, v_out,
+    op, own, away, fromcore, zin, yin, zpart, ypart, zlast, ylast, gathered, total, vsend, vin,
+    op_sem, ag_send, ag_recv, fw_send, fw_recv, core_send, core_recv,
+    rs_send, rs_recv, last_send, last_recv, v_send, v_recv,
+):
+    z, y, core = place_of()
+    x = lax.axis_index("row")
+    here = z * SIDE + y
+    other = 1 - core
+    half = (pl.ds(0, 128), pl.ds(128, 128))
+    steps = (1, 2, 3)
+
+    def load(t):
+        return pltpu.make_async_copy(op_hbm.at[t], op.at[t], op_sem.at[t])
+
+    def spot(a, b):
+        return (z - a + SIDE) % SIDE * SIDE + (y - b + SIDE) % SIDE
+
+    def gather_send(h, a, b, along):
+        piece = gathered.at[core, spot(a, b), half[h]]
+        if h == 0:
+            return remote(piece, piece, ag_send.at[h, along, b], ag_recv.at[h, along, b], clus_at(z + along, y, core))
+        return remote(piece, piece, ag_send.at[h, a, along], ag_recv.at[h, a, along], clus_at(z, y + along, core))
+
+    def gather_first(h, along):
+        piece = gathered.at[core, here, half[h]]
+        if h == 0:
+            return remote(piece, piece, ag_send.at[h, 0, along], ag_recv.at[h, 0, along], clus_at(z, y + along, core))
+        return remote(piece, piece, ag_send.at[h, along, 0], ag_recv.at[h, along, 0], clus_at(z + along, y, core))
+
+    def arrived(h, a, b):
+        piece = gathered.at[core, spot(a, b), half[h]]
+        return remote(piece, piece, ag_send.at[h, a, b], ag_recv.at[h, a, b], clus_at(z, y, other))
+
+    def forward(which, h, a, b):
+        piece = gathered.at[which, spot(a, b), half[h]]
+        return remote(piece, piece, fw_send.at[h, a, b], fw_recv.at[h, a, b], clus_at(z, y, other))
+
+    def to_core(i):
+        return remote(away.at[i], fromcore.at[i], core_send.at[i], core_recv.at[i], clus_at(z, y, other))
+
+    def scatter(h, a, b):
+        zt, yt = (z + a) % SIDE, (y + b) % SIDE
+        block = own.at[zt * SIDE + yt, half[h]]
+        if h == 0:
+            return remote(block, zin.at[a, yt], rs_send.at[h, a, b], rs_recv.at[h, a, b], clus_at(zt, y, core))
+        return remote(block, yin.at[b, zt], rs_send.at[h, a, b], rs_recv.at[h, a, b], clus_at(z, yt, core))
+
+    def scatter_last(h, along):
+        if h == 0:
+            yt = (y + along) % SIDE
+            return remote(zpart.at[yt], ylast.at[along], last_send.at[h, along], last_recv.at[h, along], clus_at(z, yt, core))
+        zt = (z + along) % SIDE
+        return remote(ypart.at[zt], zlast.at[along], last_send.at[h, along], last_recv.at[h, along], clus_at(zt, y, core))
+
+    def row_send(along):
+        xt = (x + along) % SIDE
+        return remote(vsend.at[xt], vin.at[along], v_send.at[along], v_recv.at[along], {"row": xt})
+
+    def loads(i, _):
+        load(2 * i + other).start()
+        load(2 * i + core).start()
+        return 0
+
+    lax.fori_loop(0, 16, loads, 0)
+    meet(
+        [clus_at(z, y, other)]
+        + [clus_at(z, y + d, core) for d in steps]
+        + [clus_at(z + d, y, core) for d in steps]
+        + [{"row": (x + d) % SIDE} for d in steps]
+    )
+    gathered[core, here] = q_own[...].astype(F32).T.astype(jnp.bfloat16)
+    for d in (1, 3, 2):
+        for h in range(2):
+            gather_first(h, d).start()
+    for d in (1, 3, 2):
+        for h in range(2):
+            gather_send(h, 0, 0, d).start()
+    for h in range(2):
+        forward(core, h, 0, 0).start()
+
+    def column(i, _):
+        for which, keep in ((other, away), (core, own)):
+            t = 2 * i + which
+            load(t).wait()
+            product = jnp.dot(op[t], omega[...], preferred_element_type=F32) * far[t]
+            keep[i] = product.astype(jnp.bfloat16)
+            if keep is away:
+                to_core(i).start()
+        return 0
+
+    lax.fori_loop(0, 8, column, 0)
+    for d in (1, 3, 2):
+        for h, a, b in ((0, 0, d), (1, d, 0)):
+            arrived(h, a, b).wait_recv()
+            for along in (1, 3, 2):
+                gather_send(h, a, b, along).start()
+            forward(core, h, a, b).start()
+    lax.fori_loop(8, 16, column, 0)
+
+    def pair_sum(i, _):
+        a, b = i // SIDE, i % SIDE
+        at = (z + a) % SIDE * SIDE + (y + b) % SIDE
+        to_core(at).wait_recv()
+        own[at] = (own[at].astype(F32) + fromcore[at].astype(F32)).astype(jnp.bfloat16)
+
+        @pl.when(a != 0)
+        def _():
+            scatter(0, a, b).start()
+
+        @pl.when(b != 0)
+        def _():
+            scatter(1, a, b).start()
+
+        return 0
+
+    lax.fori_loop(0, 16, pair_sum, 0)
+    total[...] = jnp.zeros_like(total)
+
+    def row_step(which, at):
+        t = 2 * at + which
+        piece = (gathered[which, at].astype(F32) * far[t]).astype(jnp.bfloat16)
+        total[...] += jnp.dot(piece, op[t], preferred_element_type=F32)
+
+    def row_own(i, _):
+        a, b = i // SIDE, i % SIDE
+
+        @pl.when(a != 0)
+        def _():
+            arrived(0, a, b).wait_recv()
+            forward(core, 0, a, b).start()
+
+        @pl.when(b != 0)
+        def _():
+            arrived(1, a, b).wait_recv()
+            forward(core, 1, a, b).start()
+
+        row_step(core, spot(a, b))
+        return 0
+
+    lax.fori_loop(0, 16, row_own, 0)
+
+    def row_other(i, _):
+        a, b = i // SIDE, i % SIDE
+        for h in range(2):
+            forward(other, h, a, b).wait_recv()
+        row_step(other, spot(a, b))
+        return 0
+
+    lax.fori_loop(0, 16, row_other, 0)
+    for quarter in range(SIDE):
+        vsend[quarter] = total[:, quarter * 256:(quarter + 1) * 256].astype(jnp.bfloat16)
+    for d in (1, 3, 2):
+        row_send(d).start()
+
+    def first_sum(i, _):
+        yt = (y + i) % SIDE
+        for d in steps:
+            scatter(0, d, i).wait_recv()
+        part = own[z * SIDE + yt, half[0]].astype(F32)
+        for d in steps:
+            part = part + zin[d, yt].astype(F32)
+        zpart[yt] = part.astype(jnp.bfloat16)
+
+        @pl.when(i == 0)
+        def _():
+            u_out[half[0], :] = part
+
+        zt = (z + i) % SIDE
+        for d in steps:
+            scatter(1, i, d).wait_recv()
+        part = own[zt * SIDE + y, half[1]].astype(F32)
+        for d in steps:
+            part = part + yin[d, zt].astype(F32)
+        ypart[zt] = part.astype(jnp.bfloat16)
+
+        @pl.when(i == 0)
+        def _():
+            u_out[half[1], :] = part
+
+        @pl.when(i != 0)
+        def _():
+            scatter_last(0, i).start()
+            scatter_last(1, i).start()
+
+        return 0
+
+    lax.fori_loop(0, SIDE, first_sum, 0)
+    for d in steps:
+        row_send(d).wait_recv()
+    share = total[:, pl.ds(pl.multiple_of(x * 256, 256), 256)]
+    for d in steps:
+        share = share + vin[d].astype(F32)
+    v_out[...] = share.T
+    for h in range(2):
+        late = (ylast, zlast)[h]
+        for d in steps:
+            scatter_last(h, d).wait_recv()
+        part = u_out[half[h], :]
+        for d in steps:
+            part = part + late[d].astype(F32)
+        u_out[half[h], :] = part
+
+    for d in steps:
+        row_send(d).wait_send()
+        for h in range(2):
+            gather_first(h, d).wait_send()
+            scatter_last(h, d).wait_send()
+
+    def drain(i, _):
+        a, b = i // SIDE, i % SIDE
+        to_core(i).wait_send()
+        for h in range(2):
+            forward(core, h, a, b).wait_send()
+
+        @pl.when(a != 0)
+        def _():
+            arrived(0, a, b).wait_send()
+            scatter(0, a, b).wait_send()
+
+        @pl.when(b != 0)
+        def _():
+            arrived(1, a, b).wait_send()
+            scatter(1, a, b).wait_send()
+
+        return 0
+
+    lax.fori_loop(0, 16, drain, 0)
+
+
+def samples_of(far, operator, omega, omega_rows):
+    vmem = pl.BlockSpec(memory_space=pltpu.VMEM)
+    bf16 = jnp.bfloat16
+    sem = pltpu.SemaphoreType.DMA
+    block = (256, 256)
+    part = (128, 256)
+    return pl.pallas_call(
+        sample_kernel,
+        out_shape=[jax.ShapeDtypeStruct(block, F32)] * 2,
+        in_specs=[pl.BlockSpec(memory_space=pltpu.SMEM), pl.BlockSpec(memory_space=pl.ANY), vmem, vmem],
+        out_specs=[vmem, vmem],
+        scratch_shapes=[
+            pltpu.VMEM(operator.shape, bf16),
+            pltpu.VMEM((16, *block), bf16),
+            pltpu.VMEM((16, *block), bf16),
+            pltpu.VMEM((16, *block), bf16),
+            pltpu.VMEM((SIDE, SIDE, *part), bf16),
+            pltpu.VMEM((SIDE, SIDE, *part), bf16),
+            pltpu.VMEM((SIDE, *part), bf16),
+            pltpu.VMEM((SIDE, *part), bf16),
+            pltpu.VMEM((SIDE, *part), bf16),
+            pltpu.VMEM((SIDE, *part), bf16),
+            pltpu.VMEM((2, 16, *block), bf16),
+            pltpu.VMEM((256, 1024), F32),
+            pltpu.VMEM((SIDE, *block), bf16),
+            pltpu.VMEM((SIDE, *block), bf16),
+            sem((32,)),
+            sem((2, SIDE, SIDE)),
+            sem((2, SIDE, SIDE)),
+            sem((2, SIDE, SIDE)),
+            sem((2, SIDE, SIDE)),
+            sem((16,)),
+            sem((16,)),
+            sem((2, SIDE, SIDE)),
+            sem((2, SIDE, SIDE)),
+            sem((2, SIDE)),
+            sem((2, SIDE)),
+            sem((SIDE,)),
+            sem((SIDE,)),
+        ],
+        compiler_params=pltpu.CompilerParams(
+            collective_id=0, has_side_effects=True, vmem_limit_bytes=48 << 20
+        ),
+        cost_estimate=pl.CostEstimate(flops=1 << 33, bytes_accessed=1 << 24, transcendentals=0),
+    )(far, operator, omega, omega_rows)
+
+
 def body(operator, omega, omega_rows, near_list):
-    cluster_count = operator.shape[0]
-    rows_share = operator.shape[1]
-    width = operator.shape[2]
     my_index = lax.axis_index("clus")
-    far = far_table(near_list, cluster_count)
+    far = far_table(near_list, operator.shape[0])
     far_mine = lax.dynamic_index_in_dim(far, my_index, 1, keepdims=False)
-    products = jnp.einsum("tij,js->tis", operator, omega, preferred_element_type=jnp.float32)
-    products = (products * far_mine[:, None, None]).astype(jnp.bfloat16)
-    received = lax.all_to_all(products, "clus", split_axis=0, concat_axis=0, tiled=True)
-    operator_rows = operator.reshape(cluster_count * rows_share, width)
-    block_part = lax.all_gather(omega_rows, "clus", axis=0, tiled=True)
-    piece_rows = block_part.shape[0]
-    owners = lax.iota(jnp.int32, piece_rows) // rows_share
-    one_hot = (owners[:, None] == lax.iota(jnp.int32, cluster_count)[None, :]).astype(jnp.float32)
-    weights = jnp.dot(one_hot, far_mine, precision=HIGHEST)
-    scaled = block_part * weights.astype(jnp.bfloat16)[:, None]
-    partial_sum = lax.dot_general(
-        operator_rows, scaled, (((0,), (0,)), ((), ())), preferred_element_type=jnp.float32
-    )
-    sample_u = jnp.sum(received.astype(jnp.float32), axis=0)
+    sample_u, share_v = samples_of(far_mine, operator, omega, omega_rows)
     leading_u = sample_u[:, :R]
     gram_u_local = local_gram(leading_u, sample_u)
-    share_v = lax.psum_scatter(partial_sum, "row", scatter_dimension=0, tiled=True)
     gram_v_local = local_gram(share_v[:, :R], share_v)
     gram_u, gram_v = lax.psum((gram_u_local, gram_v_local), "row")
     total = jnp.stack([gram_u, gram_v])

time: 218 us -> 144 us (0.66)
  waiting for transfers between devices: 131 us -> 52.4 us
  Pallas kernels: 16.7 us -> 59.8 us
  matrix products: 28.7 us -> 2.09 us
  starting transfers between devices: 16.9 us -> 7.19 us
  other arithmetic: 4 us -> 1.19 us
    all_gather x1 -> x0, waiting for transfers between devices: 57.4 us -> none  [body(): block_part = lax.all_gather(omega_rows, 'clus', axis=0, tiled=True)]
    pallas_call x0 -> x1, Pallas kernels: none -> 43.1 us  [samples_of(): pl.pallas_call(sample_kernel, out_shape=[jax.ShapeDtypeStruct(block, F32)...]
    dot_general x3 -> x0, matrix products: 25.6 us -> none  [the longest x1 12.9 us: body(): lax.dot_general(operator_rows, scaled, (((0,), (0,)), ((), ())), preferre...]
    reduce_scatter x1 -> x0, waiting for transfers between devices: 19.3 us -> none  [body(): lax.psum_scatter(partial_sum, 'row', scatter_dimension=0, tiled=True)]
    all_to_all x1 -> x0, starting transfers between devices: 9.66 us -> none  [body(): lax.all_to_all(products, 'clus', split_axis=0, concat_axis=0, tiled=True)]
    reduce_sum x1 -> x0, other arithmetic: 2.8 us -> none  [body(): sample_u = jnp.sum(received.astype(jnp.float32), axis=0)]
  transfers between devices with their start and end apart: 7 -> 4, of which waited for: 6 -> 4; matrix products, arithmetic and copies ran while one was open for 15% -> 0% of each run, Pallas kernels for 0% -> 0%
where the time goes in v2:
time: 144 us; the launch traced here: 143 us
  Pallas kernels  59.8 us (42%)
  waiting for transfers between devices  52.4 us (36%)
  between operations  14.2 us (10%)
  starting transfers between devices  7.19 us (5%)
  local copies, waits for them, and re-layouts  6.23 us (4%)
  matrix products  2.09 us (1%)
    pallas_call x1, Pallas kernels, samples_of(): pl.pallas_call(sample_kernel, out_shape=[jax.ShapeDtypeStruct(block, F32)...  43.1 us
    psum x1, waiting for transfers between devices, body(): gram_u, gram_v = lax.psum((gram_u_local, gram_v_local), 'row')  39.7 us
    pallas_call x1, Pallas kernels, factor_all(): pl.pallas_call(factor_kernel, out_shape=[jax.ShapeDtypeStruct((2, rows, R...  16.7 us
    ppermute x3, waiting for transfers between devices, partner(): lax.ppermute(x, axis, [(i, i ^ 1 << apart) for i in range(lax.axis_size(a...  12.7 us
    ppermute x3, starting transfers between devices, partner(): lax.ppermute(x, axis, [(i, i ^ 1 << apart) for i in range(lax.axis_size(a...  7.15 us
  transfers between devices with their start and end apart: 4, of which 4 were waited for; matrix products, arithmetic and copies ran while one was open for 0% of the time, Pallas kernels for 0%

profile of v2, /device:TPU:1, one launch (start us, length us, event | category | flops | bytes accessed | tf_op | source)
XLA Modules:
  0.0 143.1 jit_solution(13371029843562947852)
XLA Ops:
  7.2 0.0 all-reduce.3.cloned.1.call-start
  7.2 0.8 convert_reduce_fusion
  8.0 0.2 fusion.3.far
  8.2 0.0 copy-start
  8.2 1.0 copy-done
  9.2 0.0 copy-start.1
  9.2 0.9 copy-done.1
  10.1 43.1 %shard_map.91 = (f32[256,256]{1,0:T(8,128)S(1)}, f32[256,256]{1,0:T(8,128)S(1)}) custom-call(f32[32]{0:T(128)S(1)} %fusion.3.far, bf16[32,256,1024]{2,1,0:T(8,128)(2,1)} %op_hbm.1, bf16[1024,256]{1,0:T(8,128)(2,1)S(1)} %copy-done, bf16[256,256]{1,0:T(8,128)(2,1)S(1)} %copy-done.1), custom_call_target="tpu_custom_call" | custom-call | flops 8589934592 | bytes 16777216 | tf_op jit(solution)/shard_map/pallas_call | solution.py:388
  53.3 1.0 convolution_bitcast_fusion.1
  54.3 1.0 convolution_bitcast_fusion
  55.4 0.0 all-reduce.3.cloned.1.call-update
  55.4 39.7 %all-reduce.3.cloned.1.call-done = (f32[1,128,256]{2,1,0:T(8,128)}, f32[1,128,256]{2,1,0:T(8,128)}) async-done(((f32[1,128,256]{2,1,0:T(8,128)}, f32[1,128,256]{2,1,0:T(8,128)}), (f32[1,128,256]{2,1,0:T(8,128)}, f32[1,128,256]{2,1,0:T(8,128)})) %all-reduce.3.cloned.1.call-update) | async-done | bytes 262160 | tf_op jit(solution)/shard_map/psum | solution.py:437
  95.1 0.9 constant_dynamic-update-slice_fusion.1
  96.0 0.9 constant_dynamic-update-slice_fusion
  96.9 2.9 %collective-permute-start = (f32[2,128,256]{2,1,0:T(8,128)S(1)}, f32[2,128,256]{2,1,0:T(8,128)S(1)}, u32[]{:S(2)}, u32[]{:S(2)}) collective-permute-start(f32[2,128,256]{2,1,0:T(8,128)S(1)} %constant_dynamic-update-slice_fusion), channel_id=1, source_target_pairs={{0,4},{4,0},{8,12},{12,8},{16,20},{20,16},{24,28},{28,24},{32,36},... | collective-permute-start | bytes 786440 | tf_op jit(solution)/shard_map/ppermute | solution.py:19
  99.9 1.1 collective-permute-done
  101.0 1.3 collective-permute-start.1
  102.3 6.3 %collective-permute-done.1 = f32[2,128,256]{2,1,0:T(8,128)S(1)} collective-permute-done((f32[2,128,256]{2,1,0:T(8,128)S(1)}, f32[2,128,256]{2,1,0:T(8,128)S(1)}, u32[]{:S(2)}, u32[]{:S(2)}) %collective-permute-start.1) | collective-permute-done | bytes 262176 | tf_op jit(solution)/shard_map/ppermute | solution.py:19
  108.6 3.0 %collective-permute-start.2 = (f32[2,128,256]{2,1,0:T(8,128)S(1)}, f32[2,128,256]{2,1,0:T(8,128)S(1)}, u32[]{:S(2)}, u32[]{:S(2)}) collective-permute-start(f32[2,128,256]{2,1,0:T(8,128)S(1)} %add.19), channel_id=1, source_target_pairs={{0,16},{4,20},{8,24},{12,28},{16,0},{20,4},{24,8},{28,12},{32,48},... | collective-permute-start | bytes 786440 | tf_op jit(solution)/shard_map/ppermute | solution.py:19
  111.7 5.3 %collective-permute-done.2 = f32[2,128,256]{2,1,0:T(8,128)S(1)} collective-permute-done((f32[2,128,256]{2,1,0:T(8,128)S(1)}, f32[2,128,256]{2,1,0:T(8,128)S(1)}, u32[]{:S(2)}, u32[]{:S(2)}) %collective-permute-start.2) | collective-permute-done | bytes 262176 | tf_op jit(solution)/shard_map/ppermute | solution.py:19
  117.1 0.1 copy.14
  117.2 16.7 %shard_map.92 = (f32[2,256,128]{2,1,0:T(8,128)S(1)}, f32[2,3,256,128]{3,2,1,0:T(8,128)S(1)}, f32[2,128,256]{2,1,0:T(8,128)S(1)}) custom-call(s32[4]{0:T(128)S(1)} %shift-right-arithmetic_and_fusion.bits_ref, f32[14,128,128]{2,1,0:T(8,128)S(1)} %bitcast.31, f32[2,128,128]{2,1,0:T(8,128)S(1)} %slice.78.side_ref, f32[2,256,128]{2,1,0:T(8,128)S(1)} %pad_maximum_fusion.sample_ref), custom_call_target="tpu_custom_call" | custom-call | tf_op jit(solution)/shard_map/pallas_call | solution.py:111
  133.9 0.7 slice_bitcast_fusion.1
  134.6 0.9 fusion.4
  135.5 0.7 fusion.5
  (14 shorter events, 0.3 us)
Async XLA Ops:
  7.2 87.9 %all-reduce.3.cloned.1.call-start = ((), (), s32[]{:S(2)}) async-start(), calls=%async_computation | async-start | bytes 524288 | tf_op jit(solution)/shard_map/psum | solution.py:437
  8.2 1.0 copy-start
  9.2 0.9 copy-start.1
  96.9 4.0 %collective-permute-start = (f32[2,128,256]{2,1,0:T(8,128)S(1)}, f32[2,128,256]{2,1,0:T(8,128)S(1)}, u32[]{:S(2)}, u32[]{:S(2)}) collective-permute-start(f32[2,128,256]{2,1,0:T(8,128)S(1)} %constant_dynamic-update-slice_fusion), channel_id=1, source_target_pairs={{0,4},{4,0},{8,12},{12,8},{16,20},{20,16},{24,28},{28,24},{32,36},... | collective-permute-start | bytes 786440 | tf_op jit(solution)/shard_map/ppermute | solution.py:19
  101.0 7.6 %collective-permute-start.1 = (f32[2,128,256]{2,1,0:T(8,128)S(1)}, f32[2,128,256]{2,1,0:T(8,128)S(1)}, u32[]{:S(2)}, u32[]{:S(2)}) collective-permute-start(f32[2,128,256]{2,1,0:T(8,128)S(1)} %add.18), channel_id=1, source_target_pairs={{0,8},{4,12},{8,0},{12,4},{16,24},{20,28},{24,16},{28,20},{32,40},... | collective-permute-start | bytes 786440 | tf_op jit(solution)/shard_map/ppermute | solution.py:19
  108.6 8.4 %collective-permute-start.2 = (f32[2,128,256]{2,1,0:T(8,128)S(1)}, f32[2,128,256]{2,1,0:T(8,128)S(1)}, u32[]{:S(2)}, u32[]{:S(2)}) collective-permute-start(f32[2,128,256]{2,1,0:T(8,128)S(1)} %add.19), channel_id=1, source_target_pairs={{0,16},{4,20},{8,24},{12,28},{16,0},{20,4},{24,8},{28,12},{32,48},... | collective-permute-start | bytes 786440 | tf_op jit(solution)/shard_map/ppermute | solution.py:19
Sparse Core Ops, SparseCore 0:
  55.5 39.5 all-reduce.2

commit v3 on v2

--- a/solution.py
+++ b/solution.py
@@ -15,113 +15,6 @@
 HIGHEST = lax.Precision.HIGHEST
 
 
-def partner(x, axis, apart):
-    return lax.ppermute(x, axis, [(i, i ^ 1 << apart) for i in range(lax.axis_size(axis))])
-
-
-def far_table(near_list, cluster_count):
-    clusters = jnp.arange(cluster_count, dtype=jnp.int32)
-    matched = near_list[:, :, None] == clusters[None, None, :]
-    return 1.0 - jnp.max(matched.astype(jnp.float32), axis=1)
-
-
-def local_gram(leading, stacked):
-    return lax.dot_general(
-        leading,
-        stacked,
-        (((0,), (0,)), ((), ())),
-        precision=HIGHEST,
-        preferred_element_type=jnp.float32,
-    )
-
-
-def split3(x):
-    hi = x.astype(jnp.bfloat16).astype(F32)
-    rest = x - hi
-    mid = rest.astype(jnp.bfloat16).astype(F32)
-    low = rest - mid
-    return hi, mid, low
-
-def panel(state, m, first):
-    rows = state[m, first:first + 8, :]
-    place = lax.broadcasted_iota(jnp.int32, (8, R), 0)
-    place2 = lax.broadcasted_iota(jnp.int32, (8, 2 * R), 0)
-    cols = [jnp.broadcast_to(rows[:, first + c:first + c + 1], (8, R)) for c in range(8)]
-    for c in range(8):
-        scale = lax.rsqrt(jnp.broadcast_to(cols[c][c:c + 1, :], (8, R)))
-        mult = jnp.where(place > c, cols[c] * scale, 0.0)
-        for k in range(c + 1, 8):
-            cols[k] = cols[k] - mult * (jnp.broadcast_to(cols[k][c:c + 1, :], (8, R)) * scale)
-        scale2 = jnp.concatenate([scale, scale], axis=1)
-        mult2 = jnp.concatenate([mult, mult], axis=1)
-        pivot = jnp.broadcast_to(rows[c:c + 1, :], (8, 2 * R)) * scale2
-        rows = jnp.where(place2 == c, pivot, rows - mult2 * pivot)
-    state[m, first:first + 8, :] = rows
-    last = first + 8
-    if last < R:
-        hi, mid, low = split3(rows)
-        left = jnp.concatenate([hi, hi, mid, mid, hi, low], axis=0).astype(jnp.bfloat16)
-        right = jnp.concatenate([hi, mid, hi, mid, low, hi], axis=0).astype(jnp.bfloat16)
-        state[m, last:, :] -= lax.dot_general(left[:, last:R] if last % R == 0 else left[:, :R], right, (((0,), (0,)), ((), ())), preferred_element_type=F32)[last:, :]
-
-def chol_all(state, count):
-    for first in range(0, R, 8):
-        for m in range(count):
-            panel(state, m, first)
-
-def factor_kernel(bits_ref, gram_ref, side_ref, sample_ref, basis_ref, trans_ref, top_ref, state):
-    eye_rows = lax.broadcasted_iota(jnp.int32, (R, R), 0)
-    eye_cols = lax.broadcasted_iota(jnp.int32, (R, R), 1)
-    eye = (eye_rows == eye_cols).astype(F32)
-    count = gram_ref.shape[0]
-    for m in range(count):
-        state[m, :, :R] = gram_ref[m]
-        state[m, :, R:] = eye
-    chol_all(state, count)
-    for m in range(count):
-        state[m, :, :R] = jnp.where(eye_cols >= eye_rows, state[m, :, :R], 0.0)
-    half = count // 2
-    outer = (((1,), (1,)), ((), ()))
-    for s in range(2):
-        inverse = state[s * half + bits_ref[0], :, R:]
-        basis_ref[s] = lax.dot_general(
-            sample_ref[s], inverse, outer, precision=HIGHEST, preferred_element_type=F32
-        ) * math.sqrt(1024)
-        for k in range(MERGES):
-            at = 2 * (k + 1) + (bits_ref[k + 1] if k + 1 < MERGES else 0)
-            inverse = state[s * half + at, :, R:] * math.sqrt(2 * R)
-            for h in range(2):
-                trans_ref[s, k, h * R:(h + 1) * R, :] = lax.dot_general(
-                    state[s * half + 2 * k + h, :, :R],
-                    inverse,
-                    outer,
-                    precision=HIGHEST,
-                    preferred_element_type=F32,
-                )
-        last = s * half + 2 * MERGES
-        top_ref[s, :, :R] = state[last, :, :R] * (1.0 / math.sqrt(1024))
-        top_ref[s, :, R:] = jnp.dot(
-            state[last, :, R:], side_ref[s], precision=HIGHEST, preferred_element_type=F32
-        ) * (1.0 / math.sqrt(1024))
-
-
-def factor_all(bits, grams, side, samples):
-    vmem = pl.BlockSpec(memory_space=pltpu.VMEM)
-    count, rows = grams.shape[0], samples.shape[1]
-    return pl.pallas_call(
-        factor_kernel,
-        out_shape=[
-            jax.ShapeDtypeStruct((2, rows, R), F32),
-            jax.ShapeDtypeStruct((2, MERGES, 2 * R, R), F32),
-            jax.ShapeDtypeStruct((2, R, 2 * R), F32),
-        ],
-        in_specs=[pl.BlockSpec(memory_space=pltpu.SMEM), vmem, vmem, vmem],
-        out_specs=[vmem, vmem, vmem],
-        scratch_shapes=[pltpu.VMEM((count, R, 2 * R), F32)],
-        compiler_params=pltpu.CompilerParams(vmem_limit_bytes=40 << 20),
-    )(bits, grams, side, samples)
-
-
 SIDE = 4
 MESH = pl.DeviceIdType.MESH
 
@@ -149,10 +42,12 @@
 
 
 def sample_kernel(
-    far, op_hbm, omega, q_own, u_out, v_out,
+    near, op_hbm, omega_hbm, q_hbm, lead_out, gram_out,
     op, own, away, fromcore, zin, yin, zpart, ypart, zlast, ylast, gathered, total, vsend, vin,
     op_sem, ag_send, ag_recv, fw_send, fw_recv, core_send, core_recv,
     rs_send, rs_recv, last_send, last_recv, v_send, v_recv,
+    omega, q_own, u_sum, grams, part_in, pair_own, pair_in,
+    in_sem, part_send, part_recv, pair_send, pair_recv, spread_send, spread_recv,
 ):
     z, y, core = place_of()
     x = lax.axis_index("row")
@@ -160,6 +55,11 @@
     other = 1 - core
     half = (pl.ds(0, 128), pl.ds(128, 128))
     steps = (1, 2, 3)
+    me = lax.axis_index("clus")
+
+    def far(t):
+        is_near = (near[t, 0] == me) | (near[t, 1] == me) | (near[t, 2] == me)
+        return jnp.where(is_near, 0.0, 1.0)
 
     def load(t):
         return pltpu.make_async_copy(op_hbm.at[t], op.at[t], op_sem.at[t])
@@ -208,6 +108,52 @@
         xt = (x + along) % SIDE
         return remote(vsend.at[xt], vin.at[along], v_send.at[along], v_recv.at[along], {"row": xt})
 
+    def part_at(along, which):
+        xt = (x + along) % SIDE
+        device = {"row": xt, "clus": (here * 2 + which)}
+        return remote(
+            grams.at[which, pl.ds(pl.multiple_of(xt * 32, 32), 32)], part_in.at[along, core],
+            part_send.at[along, which], part_recv.at[along, core], device,
+        )
+
+    def part_from(along, which):
+        return remote(
+            part_in.at[along, which], part_in.at[along, which],
+            part_send.at[along, which], part_recv.at[along, which], {"row": (x - along + SIDE) % SIDE},
+        )
+
+    def pair_at(along):
+        return remote(
+            pair_own, pair_in.at[along], pair_send.at[along], pair_recv.at[along], clus_at(z, y + along, core)
+        )
+
+    def spread(stage, along, which):
+        xt = (x + along) % SIDE
+        piece = gram_out.at[core, pl.ds((0, 2)[stage], (2, 3)[stage]), pl.ds(pl.multiple_of(x * 32, 32), 32)]
+        return remote(
+            piece, piece, spread_send.at[stage, along, which], spread_recv.at[stage, along, core],
+            {"row": xt, "clus": here * 2 + which},
+        )
+
+    def spread_from(stage, along, which):
+        xs = (x - along + SIDE) % SIDE
+        piece = gram_out.at[which, pl.ds((0, 2)[stage], (2, 3)[stage]), pl.ds(pl.multiple_of(xs * 32, 32), 32)]
+        return remote(
+            piece, piece, spread_send.at[stage, along, which], spread_recv.at[stage, along, which],
+            {"row": xs},
+        )
+
+    def both_cores(act):
+        for d in (0, 1, 3, 2):
+            if d:
+                act(d, core)
+            act(d, other)
+
+    omega_in = pltpu.make_async_copy(omega_hbm, omega, in_sem.at[0])
+    q_in = pltpu.make_async_copy(q_hbm, q_own, in_sem.at[1])
+    q_in.start()
+    omega_in.start()
+
     def loads(i, _):
         load(2 * i + other).start()
         load(2 * i + core).start()
@@ -218,8 +164,9 @@
         [clus_at(z, y, other)]
         + [clus_at(z, y + d, core) for d in steps]
         + [clus_at(z + d, y, core) for d in steps]
-        + [{"row": (x + d) % SIDE} for d in steps]
+        + [{"row": (x + d) % SIDE, "clus": here * 2 + which} for d in steps for which in (core, other)]
     )
+    q_in.wait()
     gathered[core, here] = q_own[...].astype(F32).T.astype(jnp.bfloat16)
     for d in (1, 3, 2):
         for h in range(2):
@@ -230,11 +177,13 @@
     for h in range(2):
         forward(core, h, 0, 0).start()
 
+    omega_in.wait()
+
     def column(i, _):
         for which, keep in ((other, away), (core, own)):
             t = 2 * i + which
             load(t).wait()
-            product = jnp.dot(op[t], omega[...], preferred_element_type=F32) * far[t]
+            product = jnp.dot(op[t], omega[...], preferred_element_type=F32) * far(t)
             keep[i] = product.astype(jnp.bfloat16)
             if keep is away:
                 to_core(i).start()
@@ -270,7 +219,7 @@
 
     def row_step(which, at):
         t = 2 * at + which
-        piece = (gathered[which, at].astype(F32) * far[t]).astype(jnp.bfloat16)
+        piece = (gathered[which, at].astype(F32) * far(t)).astype(jnp.bfloat16)
         total[...] += jnp.dot(piece, op[t], preferred_element_type=F32)
 
     def row_own(i, _):
@@ -315,7 +264,7 @@
 
         @pl.when(i == 0)
         def _():
-            u_out[half[0], :] = part
+            u_sum[half[0], :] = part
 
         zt = (z + i) % SIDE
         for d in steps:
@@ -327,7 +276,7 @@
 
         @pl.when(i == 0)
         def _():
-            u_out[half[1], :] = part
+            u_sum[half[1], :] = part
 
         @pl.when(i != 0)
         def _():
@@ -342,16 +291,51 @@
     share = total[:, pl.ds(pl.multiple_of(x * 256, 256), 256)]
     for d in steps:
         share = share + vin[d].astype(F32)
-    v_out[...] = share.T
+    lead_out[1] = share[:R, :].T
+    grams[1] = lax.dot_general(
+        share[:R, :], share, (((1,), (1,)), ((), ())), precision=HIGHEST, preferred_element_type=F32
+    )
     for h in range(2):
         late = (ylast, zlast)[h]
         for d in steps:
             scatter_last(h, d).wait_recv()
-        part = u_out[half[h], :]
+        part = u_sum[half[h], :]
         for d in steps:
             part = part + late[d].astype(F32)
-        u_out[half[h], :] = part
-
+        u_sum[half[h], :] = part
+    lead_out[0] = u_sum[:, :R]
+    grams[0] = lax.dot_general(
+        u_sum[:, :R], u_sum[...], (((0,), (0,)), ((), ())), precision=HIGHEST, preferred_element_type=F32
+    )
+    both_cores(lambda d, which: part_at(d, which).start())
+    part_in[0, core] = grams[core, pl.ds(pl.multiple_of(x * 32, 32), 32)]
+    both_cores(lambda d, which: part_from(d, which).wait_recv())
+    my_rows = pl.ds(pl.multiple_of(x * 32, 32), 32)
+    leaf = [part_in[0, s] + part_in[1, s] + part_in[2, s] + part_in[3, s] for s in range(2)]
+    pair = leaf[0] + leaf[1]
+    pair_own[...] = pair
+    for d in (1, 3, 2):
+        pair_at(d).start()
+    for s in range(2):
+        gram_out[core, s, my_rows] = leaf[s][:, :R]
+    both_cores(lambda d, which: spread(0, d, which).start())
+    for d in steps:
+        pair_at(d).wait_recv()
+    odd = y % 2
+    near_pair = pair_in[3 - 2 * odd]
+    far_pair = pair_in[2] + pair_in[1 + 2 * odd]
+    gram_out[core, 2, my_rows] = near_pair[:, :R]
+    gram_out[core, 3, my_rows] = far_pair[:, :R]
+    gram_out[core, 4, my_rows] = ((pair + near_pair) + far_pair)[:, R:]
+    both_cores(lambda d, which: spread(1, d, which).start())
+    for stage in range(2):
+        both_cores(lambda d, which: spread_from(stage, d, which).wait_recv())
+
+    both_cores(lambda d, which: part_at(d, which).wait_send())
+    for stage in range(2):
+        both_cores(lambda d, which: spread(stage, d, which).wait_send())
+    for d in steps:
+        pair_at(d).wait_send()
     for d in steps:
         row_send(d).wait_send()
         for h in range(2):
@@ -379,16 +363,17 @@
     lax.fori_loop(0, 16, drain, 0)
 
 
-def samples_of(far, operator, omega, omega_rows):
+def grams_of(near_list, operator, omega, omega_rows):
     vmem = pl.BlockSpec(memory_space=pltpu.VMEM)
+    anywhere = pl.BlockSpec(memory_space=pl.ANY)
     bf16 = jnp.bfloat16
     sem = pltpu.SemaphoreType.DMA
     block = (256, 256)
     part = (128, 256)
     return pl.pallas_call(
         sample_kernel,
-        out_shape=[jax.ShapeDtypeStruct(block, F32)] * 2,
-        in_specs=[pl.BlockSpec(memory_space=pltpu.SMEM), pl.BlockSpec(memory_space=pl.ANY), vmem, vmem],
+        out_shape=[jax.ShapeDtypeStruct((2, 256, R), F32), jax.ShapeDtypeStruct((2, 5, R, R), F32)],
+        in_specs=[pl.BlockSpec(memory_space=pltpu.SMEM), anywhere, anywhere, anywhere],
         out_specs=[vmem, vmem],
         scratch_shapes=[
             pltpu.VMEM(operator.shape, bf16),
@@ -418,37 +403,122 @@
             sem((2, SIDE)),
             sem((SIDE,)),
             sem((SIDE,)),
+            pltpu.VMEM(omega.shape, bf16),
+            pltpu.VMEM(block, bf16),
+            pltpu.VMEM(block, F32),
+            pltpu.VMEM((2, R, 256), F32),
+            pltpu.VMEM((SIDE, 2, 32, 256), F32),
+            pltpu.VMEM((32, 256), F32),
+            pltpu.VMEM((SIDE, 32, 256), F32),
+            sem((2,)),
+            sem((SIDE, 2)),
+            sem((SIDE, 2)),
+            sem((SIDE,)),
+            sem((SIDE,)),
+            sem((2, SIDE, 2)),
+            sem((2, SIDE, 2)),
         ],
         compiler_params=pltpu.CompilerParams(
             collective_id=0, has_side_effects=True, vmem_limit_bytes=48 << 20
         ),
         cost_estimate=pl.CostEstimate(flops=1 << 33, bytes_accessed=1 << 24, transcendentals=0),
-    )(far, operator, omega, omega_rows)
+    )(near_list, operator, omega, omega_rows)
+
+
+def split3(x):
+    hi = x.astype(jnp.bfloat16).astype(F32)
+    rest = x - hi
+    mid = rest.astype(jnp.bfloat16).astype(F32)
+    low = rest - mid
+    return hi, mid, low
+
+def panel(state, m, first):
+    rows = state[m, first:first + 8, :]
+    place = lax.broadcasted_iota(jnp.int32, (8, R), 0)
+    place2 = lax.broadcasted_iota(jnp.int32, (8, 2 * R), 0)
+    cols = [jnp.broadcast_to(rows[:, first + c:first + c + 1], (8, R)) for c in range(8)]
+    for c in range(8):
+        scale = lax.rsqrt(jnp.broadcast_to(cols[c][c:c + 1, :], (8, R)))
+        mult = jnp.where(place > c, cols[c] * scale, 0.0)
+        for k in range(c + 1, 8):
+            cols[k] = cols[k] - mult * (jnp.broadcast_to(cols[k][c:c + 1, :], (8, R)) * scale)
+        scale2 = jnp.concatenate([scale, scale], axis=1)
+        mult2 = jnp.concatenate([mult, mult], axis=1)
+        pivot = jnp.broadcast_to(rows[c:c + 1, :], (8, 2 * R)) * scale2
+        rows = jnp.where(place2 == c, pivot, rows - mult2 * pivot)
+    state[m, first:first + 8, :] = rows
+    last = first + 8
+    if last < R:
+        hi, mid, low = split3(rows)
+        left = jnp.concatenate([hi, hi, mid, mid, hi, low], axis=0).astype(jnp.bfloat16)
+        right = jnp.concatenate([hi, mid, hi, mid, low, hi], axis=0).astype(jnp.bfloat16)
+        state[m, last:, :] -= lax.dot_general(left[:, last:R] if last % R == 0 else left[:, :R], right, (((0,), (0,)), ((), ())), preferred_element_type=F32)[last:, :]
+
+def chol_all(state, count):
+    for first in range(0, R, 8):
+        for m in range(count):
+            panel(state, m, first)
+
+def factor_kernel(gram_ref, lead_ref, ub_ref, vb_ref, ut_ref, vt_ref, utop_ref, vtop_ref, state):
+    _, y, core = place_of()
+    eye_rows = lax.broadcasted_iota(jnp.int32, (R, R), 0)
+    eye_cols = lax.broadcasted_iota(jnp.int32, (R, R), 1)
+    eye = (eye_rows == eye_cols).astype(F32)
+    low, high = y % 2, y // 2
+    for s in range(2):
+        at = 7 * s
+        first, second, near_pair, far_pair = (gram_ref[s, i] for i in range(4))
+        pair = first + second
+        quad = pair + near_pair
+        state[at, :, :R] = first
+        state[at + 1, :, :R] = second
+        state[at + 2 + low, :, :R] = pair
+        state[at + 3 - low, :, :R] = near_pair
+        state[at + 4 + high, :, :R] = quad
+        state[at + 5 - high, :, :R] = far_pair
+        state[at + 6, :, :R] = quad + far_pair
+        for i in range(7):
+            state[at + i, :, R:] = eye
+    chol_all(state, 14)
+    for m in range(14):
+        state[m, :, :R] = jnp.where(eye_cols >= eye_rows, state[m, :, :R], 0.0)
+    outer = (((1,), (1,)), ((), ()))
+    for s in range(2):
+        basis_ref, trans_ref, top_ref = ((ub_ref, ut_ref, utop_ref), (vb_ref, vt_ref, vtop_ref))[s]
+        at = 7 * s
+        basis_ref[...] = lax.dot_general(
+            lead_ref[s], state[at + core, :, R:] * math.sqrt(1024), outer,
+            precision=HIGHEST, preferred_element_type=F32,
+        )
+        for k in range(MERGES):
+            parent = at + (2 + low, 4 + high, 6)[k]
+            inverse = state[parent, :, R:] * math.sqrt(2 * R)
+            for h in range(2):
+                trans_ref[0, k, h * R:(h + 1) * R, :] = lax.dot_general(
+                    state[at + 2 * k + h, :, :R], inverse, outer, precision=HIGHEST, preferred_element_type=F32
+                )
+        top_ref[0, :, :R] = state[at + 6, :, :R] * (1.0 / math.sqrt(1024))
+        top_ref[0, :, R:] = jnp.dot(
+            state[at + 6, :, R:], gram_ref[s, 4], precision=HIGHEST, preferred_element_type=F32
+        ) * (1.0 / math.sqrt(1024))
+
+
+def factor_all(grams, leading):
+    vmem = pl.BlockSpec(memory_space=pltpu.VMEM)
+    shapes = [(256, R)] * 2 + [(1, MERGES, 2 * R, R)] * 2 + [(1, R, 2 * R)] * 2
+    return pl.pallas_call(
+        factor_kernel,
+        out_shape=[jax.ShapeDtypeStruct(shape, F32) for shape in shapes],
+        in_specs=[vmem, vmem],
+        out_specs=[vmem] * 6,
+        scratch_shapes=[pltpu.VMEM((14, R, 2 * R), F32)],
+        compiler_params=pltpu.CompilerParams(vmem_limit_bytes=40 << 20),
+    )(grams, leading)
 
 
 def body(operator, omega, omega_rows, near_list):
-    my_index = lax.axis_index("clus")
-    far = far_table(near_list, operator.shape[0])
-    far_mine = lax.dynamic_index_in_dim(far, my_index, 1, keepdims=False)
-    sample_u, share_v = samples_of(far_mine, operator, omega, omega_rows)
-    leading_u = sample_u[:, :R]
-    gram_u_local = local_gram(leading_u, sample_u)
-    gram_v_local = local_gram(share_v[:, :R], share_v)
-    gram_u, gram_v = lax.psum((gram_u_local, gram_v_local), "row")
-    total = jnp.stack([gram_u, gram_v])
-    ordered = []
-    for level_no in range(MERGES):
-        sibling = partner(total, "clus", level_no)
-        on_left = my_index >> level_no & 1 == 0
-        ordered.append(jnp.where(on_left, total, sibling)[:, :, :R])
-        ordered.append(jnp.where(on_left, sibling, total)[:, :, :R])
-        total = total + sibling
-    ordered.append(total[:, :, :R])
-    grams = jnp.stack(ordered, axis=1).reshape(2 * (2 * MERGES + 1), R, R)
-    bits = (my_index >> jnp.arange(4, dtype=jnp.int32)) & 1
-    samples = jnp.stack([leading_u, share_v[:, :R]])
-    basis, trans, top = factor_all(bits, grams, total[:, :, R:], samples)
-    return (basis[0], basis[1], trans[0][None], trans[1][None], top[0][None], top[1][None])
+    leading, grams = grams_of(near_list, operator, omega, omega_rows)
+    return tuple(factor_all(grams, leading))
 
 
 def solution(mesh):

time: 144 us -> 82.4 us (0.57)
  waiting for transfers between devices: 52.4 us -> 0 us
  Pallas kernels: 59.8 us -> 78.9 us
  between operations: 14.2 us -> 0.64 us
  starting transfers between devices: 7.19 us -> 0 us
  local copies, waits for them, and re-layouts: 6.23 us -> 2.71 us
  matrix products: 2.09 us -> 0 us
    psum x1 -> x0, waiting for transfers between devices: 39.7 us -> none  [body(): gram_u, gram_v = lax.psum((gram_u_local, gram_v_local), 'row')]
    pallas_call x2, Pallas kernels: 59.8 us -> 78.9 us  [the longest x1 62.2 us: grams_of(): pl.pallas_call(sample_kernel, out_shape=[jax.ShapeDtypeStruct((2, 256, R)...]
    ppermute x3 -> x0, waiting for transfers between devices: 12.7 us -> none  [partner(): lax.ppermute(x, axis, [(i, i ^ 1 << apart) for i in range(lax.axis_size(a...]
    ppermute x3 -> x0, starting transfers between devices: 7.15 us -> none  [partner(): lax.ppermute(x, axis, [(i, i ^ 1 << apart) for i in range(lax.axis_size(a...]
    dot_general x2 -> x0, matrix products: 2.09 us -> none  [local_gram(): lax.dot_general(leading, stacked, (((0,), (0,)), ((), ())), precision=HIG...]
    slice x3 -> x0, local copies, waits for them, and re-layouts: 1.65 us -> none  [the longest x1 0.93 us: body(): trans[1][None]]
  transfers between devices with their start and end apart: 4 -> 0, of which waited for: 4 -> 0; matrix products, arithmetic and copies ran while one was open for 0% -> 0% of each run, Pallas kernels for 0% -> 0%
where the time goes in v3:
time: 82.4 us; the launch traced here: 82.2 us
  Pallas kernels  78.9 us (96%)
  local copies, waits for them, and re-layouts  2.71 us (3%)
    pallas_call x1, Pallas kernels, grams_of(): pl.pallas_call(sample_kernel, out_shape=[jax.ShapeDtypeStruct((2, 256, R)...  62.2 us
    pallas_call x1, Pallas kernels, factor_all(): pl.pallas_call(factor_kernel, out_shape=[jax.ShapeDtypeStruct(shape, F32)...  16.6 us
    unnamed x5, local copies, waits for them, and re-layouts  2.71 us

profile of v3, /device:TPU:1, one launch (start us, length us, event | category | flops | bytes accessed | tf_op | source)
XLA Modules:
  0.0 82.2 jit_solution(4997455895219830266)
XLA Ops:
  0.6 0.8 copy.10.near
  1.4 0.0 copy-start
  1.4 1.0 %copy-done = bf16[1024,256]{1,0:T(8,128)(2,1)S(1)} copy-done((bf16[1024,256]{1,0:T(8,128)(2,1)S(1)}, bf16[1024,256]{1,0:T(8,128)(2,1)}, u32[]{:S(2)}) %copy-start) | copy-done | bytes 524312
  2.4 0.0 copy-start.1
  2.4 0.9 %copy-done.1 = bf16[256,256]{1,0:T(8,128)(2,1)S(1)} copy-done((bf16[256,256]{1,0:T(8,128)(2,1)S(1)}, bf16[256,256]{1,0:T(8,128)(2,1)}, u32[]{:S(2)}) %copy-start.1) | copy-done | bytes 131096
  3.3 62.2 %shard_map.91 = (f32[2,256,128]{2,1,0:T(8,128)S(1)}, f32[2,5,128,128]{3,2,1,0:T(8,128)S(1)}) custom-call(s32[32,3]{1,0:T(8,128)S(1)} %copy.10.near, bf16[32,256,1024]{2,1,0:T(8,128)(2,1)} %op_hbm.1, bf16[1024,256]{1,0:T(8,128)(2,1)S(1)} %copy-done, bf16[256,256]{1,0:T(8,128)(2,1)S(1)} %copy-done.1), custom_call_target="tpu_custom_call" | custom-call | flops 8589934592 | bytes 16777216 | tf_op jit(solution)/shard_map/pallas_call | solution.py:373
  65.6 16.6 %shard_map.92 = (f32[256,128]{1,0:T(8,128)}, f32[256,128]{1,0:T(8,128)}, f32[1,3,256,128]{3,2,1,0:T(8,128)}, f32[1,3,256,128]{3,2,1,0:T(8,128)}, f32[1,128,256]{2,1,0:T(8,128)}, /*index=5*/f32[1,128,256]{2,1,0:T(8,128)}) custom-call(f32[2,5,128,128]{3,2,1,0:T(8,128)S(1)} %get-tuple-element.8.gram_ref, f32[2,256,128]{2,1,0:T(8,128)S(1)} %get-tuple-element.9.lead_ref), custom_call_target="tpu_custom_call" | custom-call | tf_op jit(solution)/shard_map/pallas_call | solution.py:509
Async XLA Ops:
  1.4 1.0 %copy-start = (bf16[1024,256]{1,0:T(8,128)(2,1)S(1)}, bf16[1024,256]{1,0:T(8,128)(2,1)}, u32[]{:S(2)}) copy-start(bf16[1024,256]{1,0:T(8,128)(2,1)} %omega_hbm.1) | copy-start | bytes 1572868
  2.4 0.9 %copy-start.1 = (bf16[256,256]{1,0:T(8,128)(2,1)S(1)}, bf16[256,256]{1,0:T(8,128)(2,1)}, u32[]{:S(2)}) copy-start(bf16[256,256]{1,0:T(8,128)(2,1)} %q_hbm.1) | copy-start | bytes 393220

commit v4 on v1

v4 whole, which is shorter than its diff:
```python
import math

import jax
import jax.numpy as jnp
from jax import lax
from jax.experimental import pallas as pl
from jax.experimental.pallas import tpu as pltpu
from jax.sharding import PartitionSpec as P

R = 128
F32 = jnp.float32
MERGES = 3


HIGHEST = lax.Precision.HIGHEST


SIDE = 4
MESH = pl.DeviceIdType.MESH
BF16 = jnp.bfloat16
BACK = (3, 1)
EARLY = 2


def place_of():
    clus = lax.axis_index("clus")
    return (clus // 8, clus // 2 % SIDE, clus % 2)


def clus_at(z, y, core):
    return {"clus": (z % SIDE * SIDE + y % SIDE) * 2 + core}


def remote(src, dst, send, recv, device):
    return pltpu.make_async_remote_copy(
        src_ref=src, dst_ref=dst, send_sem=send, recv_sem=recv, device_id=device, device_id_type=MESH
    )


def greet(devices):
    for device in devices:
        pl.semaphore_signal(pltpu.get_barrier_semaphore(), inc=1, device_id=device, device_id_type=MESH)


def sample_kernel(
    near_hbm, op_hbm, omega_hbm, q_hbm, lead_out, gram_out,
    near, weights, op, omega, q_own, own, away, fromcore, far_in, near_in, parts, last_in, gathered, wide, total,
    vsend, vin, u_sum, grams, part_in, pair_own, pair_in,
    in_sem, op_sem, ag1_s, ag1_r, ag2_s, ag2_r, ag2x_s, ag2x_r, fw_s, fw_r, core_s, core_r,
    far_s, far_r, near_s, near_r, last_s, last_r, v_s, v_r,
    part_s, part_r, pair_s, pair_r, spread_s, spread_r, share_s, share_r,
):
    z, y, core = place_of()
    x = lax.axis_index("row")
    me = lax.axis_index("clus")
    here = z * SIDE + y
    other = 1 - core
    steps = (1, 2, 3)
    half = (pl.ds(0, 128), pl.ds(128, 128))
    pieces = tuple(tuple(pl.ds(128 * h + 64 * s, 64) for s in range(2)) for h in range(2))
    ahead = (1, 3)

    def far(t):
        return weights[pl.ds(t, 1), :]

    def spot(h, d1, d2):
        dz, dy = (d2, d1) if h == 0 else (d1, d2)
        return (z + dz) % SIDE * SIDE + (y + dy) % SIDE

    def along_y(d):
        return clus_at(z, y + d, core)

    def along_z(d):
        return clus_at(z + d, y, core)

    first = (along_y, along_z)
    second = (along_z, along_y)

    def same(ref, send, recv, device):
        return remote(ref, ref, send, recv, device)

    def ag1(h, d, d1=0):
        return same(gathered.at[core, spot(h, d1, 0), half[h]], ag1_s.at[h, d], ag1_r.at[h, d], first[h](d))

    def ag2(h, e, s, d2=0):
        return same(gathered.at[core, spot(h, e, d2), half[h]], ag2_s.at[h, e, s], ag2_r.at[h, e, s], second[h](ahead[s]))

    def ag2x(h, e, s, d2):
        return same(gathered.at[core, spot(h, e, d2), pieces[h][s]], ag2x_s.at[h, e, s], ag2x_r.at[h, e, s], second[h](ahead[s]))

    def forward(which, h, d1, d2):
        return same(gathered.at[which, spot(h, d1, d2), half[h]], fw_s.at[h, d1, d2], fw_r.at[h, d1, d2], clus_at(z, y, other))

    def to_core(i):
        return remote(away.at[i], fromcore.at[i], core_s.at[i], core_r.at[i], clus_at(z, y, other))

    def block(h, d, i):
        return (z + d) % SIDE * SIDE + i if h == 0 else i * SIDE + (y + d) % SIDE

    def far_send(h, s, i):
        return remote(own.at[block(h, 2, i), pieces[h][s]], far_in.at[h, s, i], far_s.at[h, s, i], far_r.at[h, s, i], second[h](ahead[s]))

    def near_send(h, s, i):
        return remote(own.at[block(h, ahead[s], i), half[h]], near_in.at[h, s, i], near_s.at[h, s, i], near_r.at[h, s, i], second[h](ahead[s]))

    def last_send(h, d):
        i = ((y if h == 0 else z) + d) % SIDE
        return remote(parts.at[h, i], last_in.at[h, d], last_s.at[h, d], last_r.at[h, d], first[h](d))

    def row_at(d, which=None):
        xt = (x + d) % SIDE
        return {"row": xt} if which is None else {"row": xt, "clus": here * 2 + which}

    def row_send(d):
        return remote(vsend.at[d], vin.at[d], v_s.at[d], v_r.at[d], row_at(d))

    def rows32(d):
        return pl.ds(pl.multiple_of((x + d) % SIDE * 32, 32), 32)

    def part_at(d, which):
        return remote(
            grams.at[which, rows32(d)], part_in.at[d, core], part_s.at[d, which], part_r.at[d, core], row_at(d, which)
        )

    def part_from(d, which):
        return same(part_in.at[d, which], part_s.at[d, which], part_r.at[d, which], row_at(SIDE - d))

    def pair_at(d):
        return remote(pair_own, pair_in.at[d], pair_s.at[d], pair_r.at[d], along_y(d))

    slots = (pl.ds(0, 2), pl.ds(2, 3))

    def spread(k, d, d_from=0):
        return same(gram_out.at[core, slots[k], rows32(d_from)], spread_s.at[k, d], spread_r.at[k, d], row_at(d))

    def share(which, k, d):
        return same(gram_out.at[which, slots[k], rows32(d)], share_s.at[k, d], share_r.at[k, d], clus_at(z, y, other))

    def both_cores(act):
        for d in (0, 1, 3, 2):
            if d:
                act(d, core)
            act(d, other)

    def group_at(i):
        return (z + 2 + i // 2) % SIDE * 2 + (y // 2 + 1 + i) % 2

    def load(g):
        return pltpu.make_async_copy(op_hbm.at[pl.ds(4 * g, 4)], op.at[pl.ds(4 * g, 4)], op_sem.at[g])

    partners = (
        [clus_at(z, y, other)]
        + [along_y(d) for d in steps]
        + [along_z(d) for d in steps]
        + [row_at(d, which) for d in steps for which in (core, other)]
    )
    greet(partners)
    omega_in = pltpu.make_async_copy(omega_hbm, omega, in_sem.at[0])
    q_in = pltpu.make_async_copy(q_hbm, q_own, in_sem.at[1])
    near_in_copy = pltpu.make_async_copy(near_hbm, near, in_sem.at[2])
    near_in_copy.start()
    omega_in.start()

    def start_load(i, _):
        load(group_at(i)).start()
        return 0

    lax.fori_loop(0, 8, start_load, 0)
    q_in.start()
    near_in_copy.wait()
    is_near = jnp.max((near[...] == me).astype(F32), axis=0, keepdims=True)
    count = near.shape[1]
    on_row = lax.broadcasted_iota(jnp.int32, (count, count), 0) == lax.broadcasted_iota(jnp.int32, (count, count), 1)
    near_rows = jnp.sum(jnp.where(on_row, jnp.broadcast_to(is_near, (count, count)), 0.0), axis=1, keepdims=True)
    weights[...] = jnp.broadcast_to(1.0 - near_rows, weights.shape)
    omega_in.wait()

    def begin():
        q_in.wait()
        gathered[core, here] = q_own[...].astype(F32).T.astype(BF16)
        pl.semaphore_wait(pltpu.get_barrier_semaphore(), len(partners))
        for d in (2, 1, 3):
            for h in range(2):
                ag1(h, d).start()
        for h in range(2):
            for s in range(2):
                ag2(h, 0, s).start()
        for h in range(2):
            forward(core, h, 0, 0).start()

    def first_in(d):
        for h in range(2):
            ag1(h, d, SIDE - d).wait_recv()
            for s in range(2):
                ag2(h, SIDE - d, s).start()
            forward(core, h, SIDE - d, 0).start()

    def second_in(e):
        for h in range(2):
            for s in range(2):
                ag2(h, e, s, BACK[s]).wait_recv()
                ag2x(h, e, s, BACK[s]).start()
                forward(core, h, e, BACK[s]).start()

    def second_opposite_in(e):
        for h in range(2):
            for s in range(2):
                ag2x(h, e, s, 2).wait_recv()
            forward(core, h, e, 2).start()

    def column(i):
        g = group_at(i)
        load(g).wait()
        product = jnp.dot(
            op[pl.ds(4 * g, 4)].reshape(1024, 1024), omega[...], preferred_element_type=F32
        )
        for j in range(2):
            for which in range(2):
                n = 2 * j + which
                term = (product[256 * n:256 * n + 256] * far(4 * g + n)).astype(BF16)

                @pl.when(core == which)
                def _():
                    own[2 * g + j] = term

                @pl.when(core != which)
                def _():
                    away[2 * g + j] = term


    def column_early(i, _):
        column(i)
        return 0

    def column_late(i, _):
        column(i)
        for j in range(2):
            to_core(2 * group_at(i) + j).start()
        return 0

    lax.fori_loop(0, EARLY, column_early, 0)
    begin()

    def send_early(i, _):
        for j in range(2):
            to_core(2 * group_at(i) + j).start()
        return 0

    lax.fori_loop(0, EARLY, send_early, 0)
    lax.fori_loop(EARLY, 8, column_late, 0)

    def pair_sum(i, _):
        g = group_at(i)
        for j in range(2):
            at = 2 * g + j
            to_core(at).wait_recv()
            own[at] = (own[at].astype(F32) + fromcore[at].astype(F32)).astype(BF16)
            zt, yt = at // SIDE, at % SIDE

            @pl.when(zt == (z + 2) % SIDE)
            def _():
                for s in range(2):
                    far_send(0, s, yt).start()

            @pl.when(yt == (y + 2) % SIDE)
            def _():
                for s in range(2):
                    far_send(1, s, zt).start()

        return 0

    lax.fori_loop(0, 8, pair_sum, 0)
    for d in (1, 3, 2):
        first_in(d)
    second_in(0)

    def add_far(i, _):
        for h in range(2):
            for s in range(2):
                far_send(h, s, i).wait_recv()
                at = block(h, ahead[s], i)
                own[at, pieces[h][s]] = (own[at, pieces[h][s]].astype(F32) + far_in[h, s, i].astype(F32)).astype(BF16)
                near_send(h, s, i).start()
        return 0

    lax.fori_loop(0, SIDE, add_far, 0)
    for e in (3, 1, 2):
        second_in(e)
    total[...] = jnp.zeros_like(total)

    def scaled(a, b):
        forward(other, 0, b, a).wait_recv()
        forward(other, 1, a, b).wait_recv()
        at = spot(0, b, a)
        return jnp.concatenate(
            [(gathered[which, at].astype(F32) * far(2 * at + which)).astype(BF16) for which in range(2)], axis=1
        )

    def row_step(i, _):
        a, b = i // 3 + i // 3 // 2, i % 3 + i % 3 // 2
        both = op[pl.ds(2 * spot(0, b, a), 2)].reshape(512, 1024)
        total[...] += jnp.dot(scaled(a, b), both, preferred_element_type=F32)
        return 0

    lax.fori_loop(0, 9, row_step, 0)
    for e in (0, 3, 1, 2):
        second_opposite_in(e)

    def late_place(i):
        j = i % 4
        return (2 * (1 - i // 4) + i // 4 * (j + j // 2), (1 - i // 4) * i + i // 4 * 2)

    def late_piece(i, _):
        wide[i] = scaled(*late_place(i))
        return 0

    lax.fori_loop(0, 7, late_piece, 0)

    def quarter(d):
        columns = pl.ds(pl.multiple_of((x + d) % SIDE * 256, 256), 256)

        running = total[:, columns]
        for i in range(7):
            a, b = late_place(i)
            both = op[pl.ds(2 * spot(0, b, a), 2), :, columns].reshape(512, 256)
            running = running + jnp.dot(wide[i], both, preferred_element_type=F32)
        return running

    def send_quarter(i, _):
        d = (2 + 3 * i + i // 2 * 3) % SIDE
        vsend[d] = quarter(d).astype(BF16)
        row_send(d).start()
        return 0

    def first_sum(i, _):
        for h in range(2):
            for s in range(2):
                near_send(h, s, i).wait_recv()
            part = own[block(h, 0, i), half[h]].astype(F32)
            for s in range(2):
                part = part + near_in[h, s, i].astype(F32)
            parts[h, i] = part.astype(BF16)

            @pl.when(i == (y, z)[h])
            def _():
                u_sum[half[h], :] = part

        return 0

    lax.fori_loop(0, SIDE, first_sum, 0)
    for d in (2, 1, 3):
        for h in range(2):
            last_send(h, d).start()
    lax.fori_loop(0, 3, send_quarter, 0)
    mine = quarter(0)
    for h in range(2):
        for d in steps:
            last_send(h, d).wait_recv()
        part = u_sum[half[h], :]
        for d in steps:
            part = part + last_in[h, d].astype(F32)
        u_sum[half[h], :] = part
    lead_out[0] = u_sum[:, :R]
    grams[0] = lax.dot_general(
        u_sum[:, :R], u_sum[...], (((0,), (0,)), ((), ())), precision=HIGHEST, preferred_element_type=F32
    )
    for d in (2, 1, 3):
        part_at(d, 0).start()
    for d in (2, 1, 3):
        row_send(d).wait_recv()
        mine = mine + vin[d].astype(F32)
    lead_out[1] = mine[:R, :].T
    grams[1] = lax.dot_general(
        mine[:R, :], mine, (((1,), (1,)), ((), ())), precision=HIGHEST, preferred_element_type=F32
    )
    for d in (2, 1, 3):
        part_at(d, 1).start()
    part_at(0, other).start()
    part_in[0, core] = grams[core, rows32(0)]
    both_cores(lambda d, which: part_from(d, which).wait_recv())
    leaf = [part_in[0, s] + part_in[1, s] + part_in[2, s] + part_in[3, s] for s in range(2)]
    pair = leaf[0] + leaf[1]
    pair_own[...] = pair
    for d in (2, 1, 3):
        pair_at(d).start()
    for s in range(2):
        gram_out[core, s, rows32(0)] = leaf[s][:, :R]

    def spread_out(k):
        for d in (2, 1, 3):
            spread(k, d).start()
        share(core, k, 0).start()

    def spread_in(k):
        for d in (1, 3, 2):
            spread(k, d, SIDE - d).wait_recv()
            share(core, k, SIDE - d).start()

    spread_out(0)
    for d in steps:
        pair_at(d).wait_recv()
    odd = y % 2
    near_pair = pair_in[3 - 2 * odd]
    far_pair = pair_in[2] + pair_in[1 + 2 * odd]
    gram_out[core, 2, rows32(0)] = near_pair[:, :R]
    gram_out[core, 3, rows32(0)] = far_pair[:, :R]
    gram_out[core, 4, rows32(0)] = ((pair + near_pair) + far_pair)[:, R:]
    spread_out(1)
    spread_in(0)
    spread_in(1)
    for k in range(2):
        for d in range(SIDE):
            share(other, k, d).wait_recv()

    for h in range(2):
        for s in range(2):
            for e in range(SIDE):
                ag2(h, e, s).wait_send()
                ag2x(h, e, s, BACK[s]).wait_send()

    def drain(i, _):
        for h in range(2):
            for s in range(2):
                far_send(h, s, i).wait_send()
                near_send(h, s, i).wait_send()
            for d in range(SIDE):
                forward(core, h, i, d).wait_send()
        for d in range(SIDE):
            to_core(SIDE * i + d).wait_send()
        return 0

    lax.fori_loop(0, SIDE, drain, 0)
    for d in steps:
        row_send(d).wait_send()
        for h in range(2):
            ag1(h, d).wait_send()
            last_send(h, d).wait_send()
        pair_at(d).wait_send()
    both_cores(lambda d, which: part_at(d, which).wait_send())
    for k in range(2):
        for d in steps:
            spread(k, d).wait_send()
        for d in range(SIDE):
            share(core, k, d).wait_send()


def grams_of(near_list, operator, omega, omega_rows):
    vmem = pl.BlockSpec(memory_space=pltpu.VMEM)
    sem = pltpu.SemaphoreType.DMA
    block = (256, 256)
    part = (128, 256)

    def buffer(*shape, dtype=BF16):
        return pltpu.VMEM(shape, dtype)

    def sems(*shape):
        return [sem(shape), sem(shape)]

    return pl.pallas_call(
        sample_kernel,
        out_shape=[jax.ShapeDtypeStruct((2, 256, R), F32), jax.ShapeDtypeStruct((2, 5, R, R), F32)],
        in_specs=[pl.BlockSpec(memory_space=pltpu.HBM)] * 4,
        out_specs=[vmem, vmem],
        scratch_shapes=[
            buffer(near_list.shape[1], near_list.shape[0], dtype=jnp.int32),
            buffer(operator.shape[0], 256, dtype=F32),
            buffer(*operator.shape),
            buffer(*omega.shape),
            buffer(*block),
            buffer(16, *block),
            buffer(16, *block),
            buffer(16, *block),
            buffer(2, 2, SIDE, 64, 256),
            buffer(2, 2, SIDE, *part),
            buffer(2, SIDE, *part),
            buffer(2, SIDE, *part),
            buffer(2, 16, *block),
            buffer(7, 256, 512),
            buffer(256, 1024, dtype=F32),
            buffer(SIDE, *block),
            buffer(SIDE, *block),
            buffer(*block, dtype=F32),
            buffer(2, R, 256, dtype=F32),
            buffer(SIDE, 2, 32, 256, dtype=F32),
            buffer(32, 256, dtype=F32),
            buffer(SIDE, 32, 256, dtype=F32),
            sem((3,)),
            sem((8,)),
            *sems(2, SIDE),
            *sems(2, SIDE, 2),
            *sems(2, SIDE, 2),
            *sems(2, SIDE, SIDE),
            *sems(16),
            *sems(2, 2, SIDE),
            *sems(2, 2, SIDE),
            *sems(2, SIDE),
            *sems(SIDE),
            *sems(SIDE, 2),
            *sems(SIDE),
            *sems(2, SIDE),
            *sems(2, SIDE),
        ],
        compiler_params=pltpu.CompilerParams(
            collective_id=0, has_side_effects=True, vmem_limit_bytes=52 << 20
        ),
        cost_estimate=pl.CostEstimate(flops=1 << 33, bytes_accessed=1 << 24, transcendentals=0),
    )(near_list.T, operator, omega, omega_rows)


def split3(x):
    hi = x.astype(jnp.bfloat16).astype(F32)
    rest = x - hi
    mid = rest.astype(jnp.bfloat16).astype(F32)
    low = rest - mid
    return hi, mid, low

def panel(state, m, first):
    rows = state[m, first:first + 8, :]
    place = lax.broadcasted_iota(jnp.int32, (8, R), 0)
    place2 = lax.broadcasted_iota(jnp.int32, (8, 2 * R), 0)
    cols = [jnp.broadcast_to(rows[:, first + c:first + c + 1], (8, R)) for c in range(8)]
    for c in range(8):
        scale = lax.rsqrt(jnp.broadcast_to(cols[c][c:c + 1, :], (8, R)))
        mult = jnp.where(place > c, cols[c] * scale, 0.0)
        for k in range(c + 1, 8):
            cols[k] = cols[k] - mult * (jnp.broadcast_to(cols[k][c:c + 1, :], (8, R)) * scale)
        scale2 = jnp.concatenate([scale, scale], axis=1)
        mult2 = jnp.concatenate([mult, mult], axis=1)
        pivot = jnp.broadcast_to(rows[c:c + 1, :], (8, 2 * R)) * scale2
        rows = jnp.where(place2 == c, pivot, rows - mult2 * pivot)
    state[m, first:first + 8, :] = rows
    last = first + 8
    if last < R:
        hi, mid, low = split3(rows)
        left = jnp.concatenate([hi, hi, mid, mid, hi, low], axis=0).astype(jnp.bfloat16)
        right = jnp.concatenate([hi, mid, hi, mid, low, hi], axis=0).astype(jnp.bfloat16)
        state[m, last:, :] -= lax.dot_general(left[:, last:R] if last % R == 0 else left[:, :R], right, (((0,), (0,)), ((), ())), preferred_element_type=F32)[last:, :]

def chol_all(state, count):
    for first in range(0, R, 8):
        for m in range(count):
            panel(state, m, first)

def factor_kernel(gram_ref, lead_ref, ub_ref, vb_ref, ut_ref, vt_ref, utop_ref, vtop_ref, state):
    _, y, core = place_of()
    eye_rows = lax.broadcasted_iota(jnp.int32, (R, R), 0)
    eye_cols = lax.broadcasted_iota(jnp.int32, (R, R), 1)
    eye = (eye_rows == eye_cols).astype(F32)
    low, high = y % 2, y // 2
    for s in range(2):
        at = 7 * s
        first, second, near_pair, far_pair = (gram_ref[s, i] for i in range(4))
        pair = first + second
        quad = pair + near_pair
        state[at, :, :R] = first
        state[at + 1, :, :R] = second
        state[at + 2 + low, :, :R] = pair
        state[at + 3 - low, :, :R] = near_pair
        state[at + 4 + high, :, :R] = quad
        state[at + 5 - high, :, :R] = far_pair
        state[at + 6, :, :R] = quad + far_pair
        for i in range(7):
            state[at + i, :, R:] = eye
    chol_all(state, 14)
    for m in range(14):
        state[m, :, :R] = jnp.where(eye_cols >= eye_rows, state[m, :, :R], 0.0)
    outer = (((1,), (1,)), ((), ()))
    for s in range(2):
        basis_ref, trans_ref, top_ref = ((ub_ref, ut_ref, utop_ref), (vb_ref, vt_ref, vtop_ref))[s]
        at = 7 * s
        basis_ref[...] = lax.dot_general(
            lead_ref[s], state[at + core, :, R:] * math.sqrt(1024), outer,
            precision=HIGHEST, preferred_element_type=F32,
        )
        for k in range(MERGES):
            parent = at + (2 + low, 4 + high, 6)[k]
            inverse = state[parent, :, R:] * math.sqrt(2 * R)
            for h in range(2):
                trans_ref[0, k, h * R:(h + 1) * R, :] = lax.dot_general(
                    state[at + 2 * k + h, :, :R], inverse, outer, precision=HIGHEST, preferred_element_type=F32
                )
        top_ref[0, :, :R] = state[at + 6, :, :R] * (1.0 / math.sqrt(1024))
        top_ref[0, :, R:] = jnp.dot(
            state[at + 6, :, R:], gram_ref[s, 4], precision=HIGHEST, preferred_element_type=F32
        ) * (1.0 / math.sqrt(1024))


def factor_all(grams, leading):
    vmem = pl.BlockSpec(memory_space=pltpu.VMEM)
    shapes = [(256, R)] * 2 + [(1, MERGES, 2 * R, R)] * 2 + [(1, R, 2 * R)] * 2
    return pl.pallas_call(
        factor_kernel,
        out_shape=[jax.ShapeDtypeStruct(shape, F32) for shape in shapes],
        in_specs=[vmem, vmem],
        out_specs=[vmem] * 6,
        scratch_shapes=[pltpu.VMEM((14, R, 2 * R), F32)],
        compiler_params=pltpu.CompilerParams(vmem_limit_bytes=40 << 20),
    )(grams, leading)


def body(operator, omega, omega_rows, near_list):
    leading, grams = grams_of(near_list, operator, omega, omega_rows)
    return tuple(factor_all(grams, leading))


def solution(mesh):
    in_specs = (P(None, "row", "clus"), P("clus", None), P(("clus", "row"), None), P())
    out_specs = (
        P(("clus", "row"), None),
        P(("clus", "row"), None),
        P("clus", None, None, None),
        P("clus", None, None, None),
        P("clus", None, None),
        P("clus", None, None),
    )
    return jax.shard_map(body, mesh=mesh, in_specs=in_specs, out_specs=out_specs, check_vma=False)
```

time: 218 us -> 78.2 us (0.36)
  waiting for transfers between devices: 131 us -> 0 us
  Pallas kernels: 16.7 us -> 74.8 us
  matrix products: 28.7 us -> 0 us
  starting transfers between devices: 16.9 us -> 0 us
  between operations: 13.9 us -> 0.65 us
  other arithmetic: 4 us -> 0 us
  local copies, waits for them, and re-layouts: 5.2 us -> 2.62 us
    pallas_call x1 -> x2, Pallas kernels: 16.7 us -> 74.8 us  [the longest x1 57.9 us: grams_of(): pl.pallas_call(sample_kernel, out_shape=[jax.ShapeDtypeStruct((2, 256, R)...]
    all_gather x1 -> x0, waiting for transfers between devices: 57.4 us -> none  [body(): block_part = lax.all_gather(omega_rows, 'clus', axis=0, tiled=True)]
    psum x1 -> x0, waiting for transfers between devices: 41.7 us -> none  [body(): gram_u, gram_v = lax.psum((gram_u_local, gram_v_local), 'row')]
    dot_general x5 -> x0, matrix products: 28.7 us -> none  [the longest x1 12.9 us: body(): lax.dot_general(operator_rows, scaled, (((0,), (0,)), ((), ())), preferre...]
    reduce_scatter x1 -> x0, waiting for transfers between devices: 19.3 us -> none  [body(): lax.psum_scatter(partial_sum, 'row', scatter_dimension=0, tiled=True)]
    ppermute x3 -> x0, waiting for transfers between devices: 11.8 us -> none  [partner(): lax.ppermute(x, axis, [(i, i ^ 1 << apart) for i in range(lax.axis_size(a...]
    all_to_all x1 -> x0, starting transfers between devices: 9.66 us -> none  [body(): lax.all_to_all(products, 'clus', split_axis=0, concat_axis=0, tiled=True)]
    ppermute x3 -> x0, starting transfers between devices: 7.15 us -> none  [partner(): lax.ppermute(x, axis, [(i, i ^ 1 << apart) for i in range(lax.axis_size(a...]
  transfers between devices with their start and end apart: 7 -> 0, of which waited for: 6 -> 0; matrix products, arithmetic and copies ran while one was open for 15% -> 0% of each run, Pallas kernels for 0% -> 0%
where the time goes in v4:
time: 78.2 us; the launch traced here: 78 us
  Pallas kernels  74.8 us (96%)
  local copies, waits for them, and re-layouts  2.62 us (3%)
    pallas_call x1, Pallas kernels, grams_of(): pl.pallas_call(sample_kernel, out_shape=[jax.ShapeDtypeStruct((2, 256, R)...  57.9 us
    pallas_call x1, Pallas kernels, factor_all(): pl.pallas_call(factor_kernel, out_shape=[jax.ShapeDtypeStruct(shape, F32)...  16.9 us
    unnamed x6, local copies, waits for them, and re-layouts  2.62 us

profile of v4, /device:TPU:1, one launch (start us, length us, event | category | flops | bytes accessed | tf_op | source)
XLA Modules:
  0.0 78.0 jit_solution(3299240082189982036)
XLA Ops:
  0.6 0.0 copy-start
  0.6 1.0 %copy-done = bf16[1024,256]{1,0:T(8,128)(2,1)S(1)} copy-done((bf16[1024,256]{1,0:T(8,128)(2,1)S(1)}, bf16[1024,256]{1,0:T(8,128)(2,1)}, u32[]{:S(2)}) %copy-start) | copy-done | bytes 524312
  1.7 0.0 copy-start.1
  1.7 0.9 %copy-done.1 = bf16[256,256]{1,0:T(8,128)(2,1)S(1)} copy-done((bf16[256,256]{1,0:T(8,128)(2,1)S(1)}, bf16[256,256]{1,0:T(8,128)(2,1)}, u32[]{:S(2)}) %copy-start.1) | copy-done | bytes 131096
  2.6 0.0 copy-start.2
  2.6 0.7 copy-done.2
  3.3 57.9 %shard_map.91 = (f32[2,256,128]{2,1,0:T(8,128)S(1)}, f32[2,5,128,128]{3,2,1,0:T(8,128)S(1)}) custom-call(s32[3,32]{1,0:T(4,128)S(1)} %bitcast.1, bf16[32,256,1024]{2,1,0:T(8,128)(2,1)} %op_hbm.1, bf16[1024,256]{1,0:T(8,128)(2,1)S(1)} %copy-done, bf16[256,256]{1,0:T(8,128)(2,1)S(1)} %copy-done.1), custom_call_target="tpu_custom_call" | custom-call | flops 8589934592 | bytes 16777216 | tf_op jit(solution)/shard_map/pallas_call | solution.py:459
  61.2 16.9 %shard_map.92 = (f32[256,128]{1,0:T(8,128)}, f32[256,128]{1,0:T(8,128)}, f32[1,3,256,128]{3,2,1,0:T(8,128)}, f32[1,3,256,128]{3,2,1,0:T(8,128)}, f32[1,128,256]{2,1,0:T(8,128)}, /*index=5*/f32[1,128,256]{2,1,0:T(8,128)}) custom-call(f32[2,5,128,128]{3,2,1,0:T(8,128)S(1)} %get-tuple-element.8.gram_ref, f32[2,256,128]{2,1,0:T(8,128)S(1)} %get-tuple-element.9.lead_ref), custom_call_target="tpu_custom_call" | custom-call | tf_op jit(solution)/shard_map/pallas_call | solution.py:591
Async XLA Ops:
  0.6 1.0 %copy-start = (bf16[1024,256]{1,0:T(8,128)(2,1)S(1)}, bf16[1024,256]{1,0:T(8,128)(2,1)}, u32[]{:S(2)}) copy-start(bf16[1024,256]{1,0:T(8,128)(2,1)} %omega_hbm.1) | copy-start | bytes 1572868
  1.7 0.9 %copy-start.1 = (bf16[256,256]{1,0:T(8,128)(2,1)S(1)}, bf16[256,256]{1,0:T(8,128)(2,1)}, u32[]{:S(2)}) copy-start(bf16[256,256]{1,0:T(8,128)(2,1)} %q_hbm.1) | copy-start | bytes 393220
  2.6 0.7 copy-start.2

commit v5 on v4

v5 whole, which is shorter than its diff:
```python
import math

import jax
import jax.numpy as jnp
from jax import lax
from jax.experimental import pallas as pl
from jax.experimental.pallas import tpu as pltpu
from jax.sharding import PartitionSpec as P

R = 128
F32 = jnp.float32
MERGES = 3


HIGHEST = lax.Precision.HIGHEST


SIDE = 4
MESH = pl.DeviceIdType.MESH
BF16 = jnp.bfloat16
BACK = (3, 1)
EARLY = 2


def place_of():
    clus = lax.axis_index("clus")
    return (clus // 8, clus // 2 % SIDE, clus % 2)


def clus_at(z, y, core):
    return {"clus": (z % SIDE * SIDE + y % SIDE) * 2 + core}


def remote(src, dst, send, recv, device):
    return pltpu.make_async_remote_copy(
        src_ref=src, dst_ref=dst, send_sem=send, recv_sem=recv, device_id=device, device_id_type=MESH
    )


def greet(devices):
    for device in devices:
        pl.semaphore_signal(pltpu.get_barrier_semaphore(), inc=1, device_id=device, device_id_type=MESH)


def sample_kernel(
    near_hbm, op_hbm, omega_hbm, q_hbm, lead_out, packed_out,
    near, weights, op, omega, q_own, own, away, fromcore, far_in, near_in, parts, last_in, gathered, wide, total,
    vsend, vin, u_sum, grams, part_in, pair_own, pair_in, sums, state,
    in_sem, op_sem, ag1_s, ag1_r, ag2_s, ag2_r, ag2x_s, ag2x_r, fw_s, fw_r, core_s, core_r,
    far_s, far_r, near_s, near_r, last_s, last_r, v_s, v_r,
    part_s, part_r, pair_s, pair_r, spread_s, spread_r, out_s, out_r,
):
    z, y, core = place_of()
    x = lax.axis_index("row")
    me = lax.axis_index("clus")
    here = z * SIDE + y
    other = 1 - core
    steps = (1, 2, 3)
    half = (pl.ds(0, 128), pl.ds(128, 128))
    pieces = tuple(tuple(pl.ds(128 * h + 64 * s, 64) for s in range(2)) for h in range(2))
    ahead = (1, 3)

    def far(t):
        return weights[pl.ds(t, 1), :]

    def spot(h, d1, d2):
        dz, dy = (d2, d1) if h == 0 else (d1, d2)
        return (z + dz) % SIDE * SIDE + (y + dy) % SIDE

    def along_y(d):
        return clus_at(z, y + d, core)

    def along_z(d):
        return clus_at(z + d, y, core)

    first = (along_y, along_z)
    second = (along_z, along_y)

    def same(ref, send, recv, device):
        return remote(ref, ref, send, recv, device)

    def ag1(h, d, d1=0):
        return same(gathered.at[core, spot(h, d1, 0), half[h]], ag1_s, ag1_r.at[h, d], first[h](d))

    def ag2(h, e, s, d2=0):
        return same(gathered.at[core, spot(h, e, d2), half[h]], ag2_s, ag2_r.at[h, e, s], second[h](ahead[s]))

    def ag2x(h, e, s, d2):
        return same(gathered.at[core, spot(h, e, d2), pieces[h][s]], ag2x_s, ag2x_r.at[h, e, s], second[h](ahead[s]))

    def forward(which, h, d1, d2):
        a, b = (d2, d1) if h == 0 else (d1, d2)
        return same(gathered.at[which, spot(h, d1, d2), half[h]], fw_s, fw_r.at[a, b], clus_at(z, y, other))

    def to_core(g):
        two = pl.ds(2 * g, 2)
        return remote(away.at[two], fromcore.at[two], core_s, core_r.at[g], clus_at(z, y, other))

    def wait_bytes(ref, sem):
        pltpu.make_async_copy(ref, ref, sem).wait()

    def block(h, d, i):
        return (z + d) % SIDE * SIDE + i if h == 0 else i * SIDE + (y + d) % SIDE

    def far_send(h, s, i):
        return remote(own.at[block(h, 2, i), pieces[h][s]], far_in.at[h, s, i], far_s, far_r, second[h](ahead[s]))

    def near_send(h, s, i):
        return remote(own.at[block(h, ahead[s], i), half[h]], near_in.at[h, s, i], near_s, near_r, second[h](ahead[s]))

    def last_send(h, d):
        i = ((y if h == 0 else z) + d) % SIDE
        return remote(parts.at[h, i], last_in.at[h, d], last_s, last_r.at[h], first[h](d))

    def row_at(d, which=None):
        xt = (x + d) % SIDE
        return {"row": xt} if which is None else {"row": xt, "clus": here * 2 + which}

    def row_send(d):
        return remote(vsend.at[d], vin.at[d], v_s, v_r, row_at(d))

    def rows32(d):
        return pl.ds(pl.multiple_of((x + d) % SIDE * 32, 32), 32)

    def part_at(d, which):
        return remote(grams.at[which, rows32(d)], part_in.at[2 * d + core], part_s, part_r, row_at(d, which))

    def pair_at(d):
        return remote(pair_own, pair_in.at[d], pair_s, pair_r, along_y(d))

    slots = (pl.ds(0, 2), pl.ds(2, 3))

    def spread(k, d):
        return same(sums.at[slots[k], rows32(0)], spread_s.at[k], spread_r.at[k], row_at(d))

    def group_at(i):
        return (z + 2 + i // 2) % SIDE * 2 + (y // 2 + 1 + i) % 2

    def load(g):
        return pltpu.make_async_copy(op_hbm.at[pl.ds(4 * g, 4)], op.at[pl.ds(4 * g, 4)], op_sem.at[g])

    partners = (
        [clus_at(z, y, other)]
        + [along_y(d) for d in steps]
        + [along_z(d) for d in steps]
        + [row_at(d, which) for d in steps for which in (core, other)]
    )
    greet(partners)
    omega_in = pltpu.make_async_copy(omega_hbm, omega, in_sem.at[0])
    q_in = pltpu.make_async_copy(q_hbm, q_own, in_sem.at[1])
    near_in_copy = pltpu.make_async_copy(near_hbm, near, in_sem.at[2])
    near_in_copy.start()
    omega_in.start()

    def start_load(i, _):
        load(group_at(i)).start()
        return 0

    lax.fori_loop(0, 8, start_load, 0)
    q_in.start()
    near_in_copy.wait()
    is_near = jnp.max((near[...] == me).astype(F32), axis=0, keepdims=True)
    count = near.shape[1]
    on_row = lax.broadcasted_iota(jnp.int32, (count, count), 0) == lax.broadcasted_iota(jnp.int32, (count, count), 1)
    near_rows = jnp.sum(jnp.where(on_row, jnp.broadcast_to(is_near, (count, count)), 0.0), axis=1, keepdims=True)
    weights[...] = jnp.broadcast_to(1.0 - near_rows, weights.shape)
    omega_in.wait()

    def begin():
        q_in.wait()
        gathered[core, here] = q_own[...].astype(F32).T.astype(BF16)
        pl.semaphore_wait(pltpu.get_barrier_semaphore(), len(partners))
        for d in (2, 1, 3):
            for h in range(2):
                ag1(h, d).start()
        for h in range(2):
            for s in range(2):
                ag2(h, 0, s).start()
        for h in range(2):
            forward(core, h, 0, 0).start()

    def first_in(d):
        for h in range(2):
            ag1(h, d, SIDE - d).wait_recv()
            for s in range(2):
                ag2(h, SIDE - d, s).start()
            forward(core, h, SIDE - d, 0).start()

    def second_in(e):
        for h in range(2):
            for s in range(2):
                ag2(h, e, s, BACK[s]).wait_recv()
                ag2x(h, e, s, BACK[s]).start()
                forward(core, h, e, BACK[s]).start()

    def second_opposite_in(e):
        for h in range(2):
            for s in range(2):
                ag2x(h, e, s, 2).wait_recv()
            forward(core, h, e, 2).start()

    def column(i):
        g = group_at(i)
        load(g).wait()
        product = jnp.dot(
            op[pl.ds(4 * g, 4)].reshape(1024, 1024), omega[...], preferred_element_type=F32
        )
        for j in range(2):
            for which in range(2):
                n = 2 * j + which
                term = (product[256 * n:256 * n + 256] * far(4 * g + n)).astype(BF16)

                @pl.when(core == which)
                def _():
                    own[2 * g + j] = term

                @pl.when(core != which)
                def _():
                    away[2 * g + j] = term


    def column_early(i, _):
        column(i)
        return 0

    def column_late(i, _):
        column(i)
        to_core(group_at(i)).start()
        return 0

    lax.fori_loop(0, EARLY, column_early, 0)
    begin()

    def send_early(i, _):
        to_core(group_at(i)).start()
        return 0

    lax.fori_loop(0, EARLY, send_early, 0)
    lax.fori_loop(EARLY, 8, column_late, 0)

    def pair_sum(i, _):
        g = group_at(i)
        to_core(g).wait_recv()
        for j in range(2):
            at = 2 * g + j
            own[at] = (own[at].astype(F32) + fromcore[at].astype(F32)).astype(BF16)
            zt, yt = at // SIDE, at % SIDE

            @pl.when(zt == (z + 2) % SIDE)
            def _():
                for s in range(2):
                    far_send(0, s, yt).start()

            @pl.when(yt == (y + 2) % SIDE)
            def _():
                for s in range(2):
                    far_send(1, s, zt).start()

        return 0

    lax.fori_loop(0, 8, pair_sum, 0)
    for d in (1, 3, 2):
        first_in(d)
    second_in(0)

    wait_bytes(far_in, far_r)

    def add_far(i, _):
        for h in range(2):
            for s in range(2):
                at = block(h, ahead[s], i)
                own[at, pieces[h][s]] = (own[at, pieces[h][s]].astype(F32) + far_in[h, s, i].astype(F32)).astype(BF16)
                near_send(h, s, i).start()
        return 0

    lax.fori_loop(0, SIDE, add_far, 0)
    for e in (3, 1, 2):
        second_in(e)
    total[...] = jnp.zeros_like(total)

    def scaled(a, b):
        at = spot(0, b, a)
        wait_bytes(gathered.at[other, at], fw_r.at[a, b])
        return jnp.concatenate(
            [(gathered[which, at].astype(F32) * far(2 * at + which)).astype(BF16) for which in range(2)], axis=1
        )

    def row_step(i, _):
        a, b = i // 3 + i // 3 // 2, i % 3 + i % 3 // 2
        both = op[pl.ds(2 * spot(0, b, a), 2)].reshape(512, 1024)
        total[...] += jnp.dot(scaled(a, b), both, preferred_element_type=F32)
        return 0

    lax.fori_loop(0, 9, row_step, 0)
    for e in (0, 3, 1, 2):
        second_opposite_in(e)

    def late_place(i):
        j = i % 4
        return (2 * (1 - i // 4) + i // 4 * (j + j // 2), (1 - i // 4) * i + i // 4 * 2)

    def late_piece(i, _):
        wide[i] = scaled(*late_place(i))
        return 0

    lax.fori_loop(0, 7, late_piece, 0)

    def quarter(d):
        columns = pl.ds(pl.multiple_of((x + d) % SIDE * 256, 256), 256)

        running = total[:, columns]
        for i in range(7):
            a, b = late_place(i)
            both = op[pl.ds(2 * spot(0, b, a), 2), :, columns].reshape(512, 256)
            running = running + jnp.dot(wide[i], both, preferred_element_type=F32)
        return running

    def send_quarter(i, _):
        d = (2 + 3 * i + i // 2 * 3) % SIDE
        vsend[d] = quarter(d).astype(BF16)
        row_send(d).start()
        return 0

    wait_bytes(near_in, near_r)

    def first_sum(i, _):
        for h in range(2):
            part = own[block(h, 0, i), half[h]].astype(F32)
            for s in range(2):
                part = part + near_in[h, s, i].astype(F32)
            parts[h, i] = part.astype(BF16)

            @pl.when(i == (y, z)[h])
            def _():
                u_sum[half[h], :] = part

        return 0

    lax.fori_loop(0, SIDE, first_sum, 0)
    for d in (2, 1, 3):
        for h in range(2):
            last_send(h, d).start()
    lax.fori_loop(0, 3, send_quarter, 0)
    mine = quarter(0)
    for h in range(2):
        wait_bytes(last_in.at[h, pl.ds(1, 3)], last_r.at[h])
        part = u_sum[half[h], :]
        for d in steps:
            part = part + last_in[h, d].astype(F32)
        u_sum[half[h], :] = part
    lead_out[0] = u_sum[:, :R]
    grams[0] = lax.dot_general(
        u_sum[:, :R], u_sum[...], (((0,), (0,)), ((), ())), precision=HIGHEST, preferred_element_type=F32
    )
    for d in (2, 1, 3):
        part_at(d, 0).start()
    wait_bytes(vin.at[pl.ds(1, 3)], v_r)
    for d in steps:
        mine = mine + vin[d].astype(F32)
    lead_out[1] = mine[:R, :].T
    grams[1] = lax.dot_general(
        mine[:R, :], mine, (((1,), (1,)), ((), ())), precision=HIGHEST, preferred_element_type=F32
    )
    for d in (2, 1, 3):
        part_at(d, 1).start()
    part_at(0, other).start()
    part_in[core] = grams[core, rows32(0)]
    wait_bytes(part_in.at[pl.ds(1, 7)], part_r)
    leaf = [part_in[s] + part_in[2 + s] + part_in[4 + s] + part_in[6 + s] for s in range(2)]
    pair = leaf[0] + leaf[1]
    pair_own[...] = pair
    for d in (2, 1, 3):
        pair_at(d).start()
    for s in range(2):
        sums[s, rows32(0)] = leaf[s][:, :R]
    for d in (2, 1, 3):
        spread(0, d).start()
    wait_bytes(pair_in.at[pl.ds(1, 3)], pair_r)
    low, high = y % 2, y // 2
    near_pair = pair_in[3 - 2 * low]
    far_pair = pair_in[2] + pair_in[1 + 2 * low]
    sums[2, rows32(0)] = near_pair[:, :R]
    sums[3, rows32(0)] = far_pair[:, :R]
    sums[4, rows32(0)] = ((pair + near_pair) + far_pair)[:, R:]
    for d in (2, 1, 3):
        spread(1, d).start()
    spread_size = [sums.at[slots[k], pl.ds(0, 96)] for k in range(2)]
    for k in range(2):
        wait_bytes(spread_size[k], spread_r.at[k])

    pair = sums[0] + sums[1]
    quad = pair + sums[2]
    state[0] = sums[0]
    state[1] = sums[1]
    state[2 + low] = pair
    state[3 - low] = sums[2]
    state[4 + high] = quad
    state[5 - high] = sums[3]
    state[6] = quad + sums[3]
    state[7] = sums[4]
    chol_all(state, 7)
    result = remote(state, packed_out.at[core], out_s, out_r, clus_at(z, y, other))
    result.start()
    packed_out[core] = state[...]
    result.wait_recv()

    result.wait_send()
    for ref, sem in (
        (gathered.at[0, pl.ds(0, 3)], ag1_s),
        (gathered.at[0, pl.ds(0, 8)], ag2_s),
        (gathered.at[0, pl.ds(0, 4)], ag2x_s),
        (gathered.at[0], fw_s),
        (away, core_s),
        (far_in, far_s),
        (near_in, near_s),
        (gathered.at[0, pl.ds(0, 3)], last_s),
        (vin.at[pl.ds(1, 3)], v_s),
        (part_in.at[pl.ds(1, 7)], part_s),
        (pair_in.at[pl.ds(1, 3)], pair_s),
        (spread_size[0], spread_s.at[0]),
        (spread_size[1], spread_s.at[1]),
    ):
        wait_bytes(ref, sem)


def grams_of(near_list, operator, omega, omega_rows):
    vmem = pl.BlockSpec(memory_space=pltpu.VMEM)
    sem = pltpu.SemaphoreType.DMA
    block = (256, 256)
    part = (128, 256)

    def buffer(*shape, dtype=BF16):
        return pltpu.VMEM(shape, dtype)

    one = sem(())

    return pl.pallas_call(
        sample_kernel,
        out_shape=[jax.ShapeDtypeStruct((2, 256, R), F32), jax.ShapeDtypeStruct((2, 8, R, R), F32)],
        in_specs=[pl.BlockSpec(memory_space=pltpu.HBM)] * 4,
        out_specs=[vmem, vmem],
        scratch_shapes=[
            buffer(near_list.shape[1], near_list.shape[0], dtype=jnp.int32),
            buffer(operator.shape[0], 256, dtype=F32),
            buffer(*operator.shape),
            buffer(*omega.shape),
            buffer(*block),
            buffer(16, *block),
            buffer(16, *block),
            buffer(16, *block),
            buffer(2, 2, SIDE, 64, 256),
            buffer(2, 2, SIDE, *part),
            buffer(2, SIDE, *part),
            buffer(2, SIDE, *part),
            buffer(2, 16, *block),
            buffer(7, 256, 512),
            buffer(256, 1024, dtype=F32),
            buffer(SIDE, *block),
            buffer(SIDE, *block),
            buffer(*block, dtype=F32),
            buffer(2, R, 256, dtype=F32),
            buffer(8, 32, 256, dtype=F32),
            buffer(32, 256, dtype=F32),
            buffer(SIDE, 32, 256, dtype=F32),
            buffer(5, R, R, dtype=F32),
            buffer(8, R, R, dtype=F32),
            sem((3,)),
            sem((8,)),
            one,
            sem((2, SIDE)),
            one,
            sem((2, SIDE, 2)),
            one,
            sem((2, SIDE, 2)),
            one,
            sem((SIDE, SIDE)),
            one,
            sem((8,)),
            one,
            one,
            one,
            one,
            one,
            sem((2,)),
            one,
            one,
            one,
            one,
            one,
            one,
            sem((2,)),
            sem((2,)),
            one,
            one,
        ],
        compiler_params=pltpu.CompilerParams(
            collective_id=0, has_side_effects=True, vmem_limit_bytes=52 << 20
        ),
        cost_estimate=pl.CostEstimate(flops=1 << 33, bytes_accessed=1 << 24, transcendentals=0),
    )(near_list.T, operator, omega, omega_rows)


def split3(x):
    hi = x.astype(jnp.bfloat16).astype(F32)
    rest = x - hi
    mid = rest.astype(jnp.bfloat16).astype(F32)
    low = rest - mid
    return hi, mid, low


def panel(state, m, first):
    last = first + 8
    rows = state[m, first:last, :]
    place = lax.broadcasted_iota(jnp.int32, (8, R), 0)
    lane = lax.broadcasted_iota(jnp.int32, (8, R), 1)
    cols = [jnp.broadcast_to(rows[:, first + c:first + c + 1], (8, R)) for c in range(8)]
    for c in range(8):
        scale = lax.rsqrt(jnp.broadcast_to(cols[c][c:c + 1, :], (8, R)))
        mult = jnp.where(place > c, cols[c] * scale, 0.0)
        for k in range(c + 1, 8):
            cols[k] = cols[k] - mult * (jnp.broadcast_to(cols[k][c:c + 1, :], (8, R)) * scale)
        pivot = jnp.where(lane == first + c, 1.0, jnp.broadcast_to(rows[c:c + 1, :], (8, R))) * scale
        kept = jnp.where((lane == first + c) & (place > c), 0.0, rows)
        rows = jnp.where(place == c, pivot, kept - mult * pivot)
    state[m, first:last, :] = rows
    if last < R:
        hi, mid, low = split3(rows)
        left = jnp.concatenate([hi, hi, mid, mid, hi, low], axis=0).astype(jnp.bfloat16)
        hi, mid, low = (jnp.where((lane < last) & (lane - first > place), 0.0, part) for part in (hi, mid, low))
        right = jnp.concatenate([hi, mid, hi, mid, low, hi], axis=0).astype(jnp.bfloat16)
        update = lax.dot_general(left, right, (((0,), (0,)), ((), ())), preferred_element_type=F32)
        below = lax.broadcasted_iota(jnp.int32, (R - last, R), 1)
        cleared = jnp.where((below >= first) & (below < last), 0.0, state[m, last:, :])
        state[m, last:, :] = cleared - update[last:, :]


def chol_all(state, count):
    for first in range(0, R, 8):
        for m in range(count):
            panel(state, m, first)


def upper_of(packed):
    row = lax.broadcasted_iota(jnp.int32, (R, R), 0)
    col = lax.broadcasted_iota(jnp.int32, (R, R), 1)
    return jnp.where(col > row, packed, jnp.where(col == row, 1.0 / packed, 0.0))


def inverse_of(packed):
    row = lax.broadcasted_iota(jnp.int32, (R, R), 0)
    col = lax.broadcasted_iota(jnp.int32, (R, R), 1)
    return jnp.where(col <= row, packed, 0.0)


def output_kernel(packed, lead_ref, ub_ref, vb_ref, ut_ref, vt_ref, utop_ref, vtop_ref):
    _, y, core = place_of()
    outer = (((1,), (1,)), ((), ()))
    for s in range(2):
        basis_ref, trans_ref, top_ref = ((ub_ref, ut_ref, utop_ref), (vb_ref, vt_ref, vtop_ref))[s]
        basis_ref[...] = lax.dot_general(
            lead_ref[s], inverse_of(packed[s, core]) * math.sqrt(1024), outer,
            precision=HIGHEST, preferred_element_type=F32,
        )
        for k in range(MERGES):
            inverse = inverse_of(packed[s, (2 + y % 2, 4 + y // 2, 6)[k]]) * math.sqrt(2 * R)
            for h in range(2):
                trans_ref[0, k, h * R:(h + 1) * R, :] = lax.dot_general(
                    upper_of(packed[s, 2 * k + h]), inverse, outer, precision=HIGHEST, preferred_element_type=F32
                )
        top_ref[0, :, :R] = upper_of(packed[s, 6]) * (1.0 / math.sqrt(1024))
        top_ref[0, :, R:] = jnp.dot(
            inverse_of(packed[s, 6]), packed[s, 7], precision=HIGHEST, preferred_element_type=F32
        ) * (1.0 / math.sqrt(1024))


def outputs_of(packed, leading):
    vmem = pl.BlockSpec(memory_space=pltpu.VMEM)
    shapes = [(256, R)] * 2 + [(1, MERGES, 2 * R, R)] * 2 + [(1, R, 2 * R)] * 2
    return pl.pallas_call(
        output_kernel,
        out_shape=[jax.ShapeDtypeStruct(shape, F32) for shape in shapes],
        in_specs=[vmem, vmem],
        out_specs=[vmem] * 6,
        compiler_params=pltpu.CompilerParams(vmem_limit_bytes=40 << 20),
    )(packed, leading)


def body(operator, omega, omega_rows, near_list):
    leading, packed = grams_of(near_list, operator, omega, omega_rows)
    return tuple(outputs_of(packed, leading))


def solution(mesh):
    in_specs = (P(None, "row", "clus"), P("clus", None), P(("clus", "row"), None), P())
    out_specs = (
        P(("clus", "row"), None),
        P(("clus", "row"), None),
        P("clus", None, None, None),
        P("clus", None, None, None),
        P("clus", None, None),
        P("clus", None, None),
    )
    return jax.shard_map(body, mesh=mesh, in_specs=in_specs, out_specs=out_specs, check_vma=False)
```

time: 78.2 us -> 70.8 us (0.905)
  Pallas kernels: 74.8 us -> 67.3 us
    pallas_call x1, Pallas kernels: 16.9 us -> 2.67 us  [outputs_of(): pl.pallas_call(output_kernel, out_shape=[jax.ShapeDtypeStruct(shape, F32)...]
    pallas_call x1, Pallas kernels: 57.9 us -> 64.6 us  [grams_of(): pl.pallas_call(sample_kernel, out_shape=[jax.ShapeDtypeStruct((2, 256, R)...]
where the time goes in v5:
time: 70.8 us; the launch traced here: 70.6 us
  Pallas kernels  67.3 us (95%)
  local copies, waits for them, and re-layouts  2.62 us (4%)
    pallas_call x1, Pallas kernels, grams_of(): pl.pallas_call(sample_kernel, out_shape=[jax.ShapeDtypeStruct((2, 256, R)...  64.6 us
    pallas_call x1, Pallas kernels, outputs_of(): pl.pallas_call(output_kernel, out_shape=[jax.ShapeDtypeStruct(shape, F32)...  2.67 us
    unnamed x6, local copies, waits for them, and re-layouts  2.62 us

profile of v5, /device:TPU:1, one launch (start us, length us, event | category | flops | bytes accessed | tf_op | source)
XLA Modules:
  0.0 70.6 jit_solution(1060324195360701847)
XLA Ops:
  0.6 0.0 copy-start
  0.6 1.0 %copy-done = bf16[1024,256]{1,0:T(8,128)(2,1)S(1)} copy-done((bf16[1024,256]{1,0:T(8,128)(2,1)S(1)}, bf16[1024,256]{1,0:T(8,128)(2,1)}, u32[]{:S(2)}) %copy-start) | copy-done | bytes 524312
  1.7 0.0 copy-start.1
  1.7 0.9 %copy-done.1 = bf16[256,256]{1,0:T(8,128)(2,1)S(1)} copy-done((bf16[256,256]{1,0:T(8,128)(2,1)S(1)}, bf16[256,256]{1,0:T(8,128)(2,1)}, u32[]{:S(2)}) %copy-start.1) | copy-done | bytes 131096
  2.6 0.0 copy-start.2
  2.6 0.7 copy-done.2
  3.3 64.6 %shard_map.91 = (f32[2,256,128]{2,1,0:T(8,128)S(1)}, f32[2,8,128,128]{3,2,1,0:T(8,128)S(1)}) custom-call(s32[3,32]{1,0:T(4,128)S(1)} %bitcast.1, bf16[32,256,1024]{2,1,0:T(8,128)(2,1)} %op_hbm.1, bf16[1024,256]{1,0:T(8,128)(2,1)S(1)} %copy-done, bf16[256,256]{1,0:T(8,128)(2,1)S(1)} %copy-done.1), custom_call_target="tpu_custom_call" | custom-call | flops 8589934592 | bytes 16777216 | tf_op jit(solution)/shard_map/pallas_call | solution.py:437
  67.9 2.7 %shard_map.92 = (f32[256,128]{1,0:T(8,128)}, f32[256,128]{1,0:T(8,128)}, f32[1,3,256,128]{3,2,1,0:T(8,128)}, f32[1,3,256,128]{3,2,1,0:T(8,128)}, f32[1,128,256]{2,1,0:T(8,128)}, /*index=5*/f32[1,128,256]{2,1,0:T(8,128)}) custom-call(f32[2,8,128,128]{3,2,1,0:T(8,128)S(1)} %get-tuple-element.8.packed, f32[2,256,128]{2,1,0:T(8,128)S(1)} %get-tuple-element.9.lead_ref), custom_call_target="tpu_custom_call" | custom-call | tf_op jit(solution)/shard_map/pallas_call | solution.py:579
Async XLA Ops:
  0.6 1.0 %copy-start = (bf16[1024,256]{1,0:T(8,128)(2,1)S(1)}, bf16[1024,256]{1,0:T(8,128)(2,1)}, u32[]{:S(2)}) copy-start(bf16[1024,256]{1,0:T(8,128)(2,1)} %omega_hbm.1) | copy-start | bytes 1572868
  1.7 0.9 %copy-start.1 = (bf16[256,256]{1,0:T(8,128)(2,1)S(1)}, bf16[256,256]{1,0:T(8,128)(2,1)}, u32[]{:S(2)}) copy-start(bf16[256,256]{1,0:T(8,128)(2,1)} %q_hbm.1) | copy-start | bytes 393220
  2.6 0.7 copy-start.2

commit v6 on v5

--- a/solution.py
+++ b/solution.py
@@ -236,7 +236,10 @@
         return 0
 
     lax.fori_loop(0, EARLY, send_early, 0)
-    lax.fori_loop(EARLY, 8, column_late, 0)
+    lax.fori_loop(EARLY, 6, column_late, 0)
+    for d in (1, 3, 2):
+        first_in(d)
+    lax.fori_loop(6, 8, column_late, 0)
 
     def pair_sum(i, _):
         g = group_at(i)
@@ -259,23 +262,7 @@
         return 0
 
     lax.fori_loop(0, 8, pair_sum, 0)
-    for d in (1, 3, 2):
-        first_in(d)
     second_in(0)
-
-    wait_bytes(far_in, far_r)
-
-    def add_far(i, _):
-        for h in range(2):
-            for s in range(2):
-                at = block(h, ahead[s], i)
-                own[at, pieces[h][s]] = (own[at, pieces[h][s]].astype(F32) + far_in[h, s, i].astype(F32)).astype(BF16)
-                near_send(h, s, i).start()
-        return 0
-
-    lax.fori_loop(0, SIDE, add_far, 0)
-    for e in (3, 1, 2):
-        second_in(e)
     total[...] = jnp.zeros_like(total)
 
     def scaled(a, b):
@@ -285,13 +272,29 @@
             [(gathered[which, at].astype(F32) * far(2 * at + which)).astype(BF16) for which in range(2)], axis=1
         )
 
-    def row_step(i, _):
-        a, b = i // 3 + i // 3 // 2, i % 3 + i % 3 // 2
+    def row_step(a, b):
         both = op[pl.ds(2 * spot(0, b, a), 2)].reshape(512, 1024)
         total[...] += jnp.dot(scaled(a, b), both, preferred_element_type=F32)
         return 0
 
-    lax.fori_loop(0, 9, row_step, 0)
+    lax.fori_loop(0, 3, lambda i, _: row_step(0, i + i // 2), 0)
+    lax.fori_loop(0, 2, lambda i, _: row_step(1 + 2 * i, 0), 0)
+    second_in(3)
+    second_in(1)
+    second_in(2)
+
+    wait_bytes(far_in, far_r)
+
+    def add_far(i, _):
+        for h in range(2):
+            for s in range(2):
+                at = block(h, ahead[s], i)
+                own[at, pieces[h][s]] = (own[at, pieces[h][s]].astype(F32) + far_in[h, s, i].astype(F32)).astype(BF16)
+                near_send(h, s, i).start()
+        return 0
+
+    lax.fori_loop(0, SIDE, add_far, 0)
+    lax.fori_loop(0, 4, lambda i, _: row_step(1 + i // 2 * 2, 1 + i % 2 * 2), 0)
     for e in (0, 3, 1, 2):
         second_opposite_in(e)
 
@@ -321,6 +324,8 @@
         row_send(d).start()
         return 0
 
+    lax.fori_loop(0, 3, send_quarter, 0)
+
     wait_bytes(near_in, near_r)
 
     def first_sum(i, _):
@@ -340,7 +345,6 @@
     for d in (2, 1, 3):
         for h in range(2):
             last_send(h, d).start()
-    lax.fori_loop(0, 3, send_quarter, 0)
     mine = quarter(0)
     for h in range(2):
         wait_bytes(last_in.at[h, pl.ds(1, 3)], last_r.at[h])
@@ -516,12 +520,12 @@
     cols = [jnp.broadcast_to(rows[:, first + c:first + c + 1], (8, R)) for c in range(8)]
     for c in range(8):
         scale = lax.rsqrt(jnp.broadcast_to(cols[c][c:c + 1, :], (8, R)))
-        mult = jnp.where(place > c, cols[c] * scale, 0.0)
+        mult = jnp.where(place > c, cols[c] * (scale * scale), 0.0)
         for k in range(c + 1, 8):
-            cols[k] = cols[k] - mult * (jnp.broadcast_to(cols[k][c:c + 1, :], (8, R)) * scale)
-        pivot = jnp.where(lane == first + c, 1.0, jnp.broadcast_to(rows[c:c + 1, :], (8, R))) * scale
+            cols[k] = cols[k] - mult * jnp.broadcast_to(cols[k][c:c + 1, :], (8, R))
+        pivot = jnp.where(lane == first + c, 1.0, jnp.broadcast_to(rows[c:c + 1, :], (8, R)))
         kept = jnp.where((lane == first + c) & (place > c), 0.0, rows)
-        rows = jnp.where(place == c, pivot, kept - mult * pivot)
+        rows = jnp.where(place == c, pivot * scale, kept - mult * pivot)
     state[m, first:last, :] = rows
     if last < R:
         hi, mid, low = split3(rows)

time: 70.8 us -> 67 us (0.946)
  Pallas kernels: 67.3 us -> 63.5 us
    pallas_call x1, Pallas kernels: 64.6 us -> 60.8 us  [grams_of(): pl.pallas_call(sample_kernel, out_shape=[jax.ShapeDtypeStruct((2, 256, R)...]
where the time goes in v6:
time: 67 us; the launch traced here: 66.8 us
  Pallas kernels  63.5 us (95%)
  local copies, waits for them, and re-layouts  2.62 us (4%)
    pallas_call x1, Pallas kernels, grams_of(): pl.pallas_call(sample_kernel, out_shape=[jax.ShapeDtypeStruct((2, 256, R)...  60.8 us
    pallas_call x1, Pallas kernels, outputs_of(): pl.pallas_call(output_kernel, out_shape=[jax.ShapeDtypeStruct(shape, F32)...  2.67 us
    unnamed x6, local copies, waits for them, and re-layouts  2.62 us

profile of v6, /device:TPU:1, one launch (start us, length us, event | category | flops | bytes accessed | tf_op | source)
XLA Modules:
  0.0 66.8 jit_solution(5666127460714192841)
XLA Ops:
  0.6 0.0 copy-start
  0.6 1.0 %copy-done = bf16[1024,256]{1,0:T(8,128)(2,1)S(1)} copy-done((bf16[1024,256]{1,0:T(8,128)(2,1)S(1)}, bf16[1024,256]{1,0:T(8,128)(2,1)}, u32[]{:S(2)}) %copy-start) | copy-done | bytes 524312
  1.7 0.0 copy-start.1
  1.7 0.9 %copy-done.1 = bf16[256,256]{1,0:T(8,128)(2,1)S(1)} copy-done((bf16[256,256]{1,0:T(8,128)(2,1)S(1)}, bf16[256,256]{1,0:T(8,128)(2,1)}, u32[]{:S(2)}) %copy-start.1) | copy-done | bytes 131096
  2.6 0.0 copy-start.2
  2.6 0.7 %copy-done.2 = s32[32,3]{0,1:T(4,128)S(1)} copy-done((s32[32,3]{0,1:T(4,128)S(1)}, s32[32,3]{0,1:T(4,128)}, u32[]{:S(2)}) %copy-start.2) | copy-done | bytes 408
  3.3 60.8 %shard_map.91 = (f32[2,256,128]{2,1,0:T(8,128)S(1)}, f32[2,8,128,128]{3,2,1,0:T(8,128)S(1)}) custom-call(s32[3,32]{1,0:T(4,128)S(1)} %bitcast.1, bf16[32,256,1024]{2,1,0:T(8,128)(2,1)} %op_hbm.1, bf16[1024,256]{1,0:T(8,128)(2,1)S(1)} %copy-done, bf16[256,256]{1,0:T(8,128)(2,1)S(1)} %copy-done.1), custom_call_target="tpu_custom_call" | custom-call | flops 8589934592 | bytes 16777216 | tf_op jit(solution)/shard_map/pallas_call | solution.py:441
  64.1 2.7 %shard_map.92 = (f32[256,128]{1,0:T(8,128)}, f32[256,128]{1,0:T(8,128)}, f32[1,3,256,128]{3,2,1,0:T(8,128)}, f32[1,3,256,128]{3,2,1,0:T(8,128)}, f32[1,128,256]{2,1,0:T(8,128)}, /*index=5*/f32[1,128,256]{2,1,0:T(8,128)}) custom-call(f32[2,8,128,128]{3,2,1,0:T(8,128)S(1)} %get-tuple-element.8.packed, f32[2,256,128]{2,1,0:T(8,128)S(1)} %get-tuple-element.9.lead_ref), custom_call_target="tpu_custom_call" | custom-call | tf_op jit(solution)/shard_map/pallas_call | solution.py:583
Async XLA Ops:
  0.6 1.0 %copy-start = (bf16[1024,256]{1,0:T(8,128)(2,1)S(1)}, bf16[1024,256]{1,0:T(8,128)(2,1)}, u32[]{:S(2)}) copy-start(bf16[1024,256]{1,0:T(8,128)(2,1)} %omega_hbm.1) | copy-start | bytes 1572868
  1.7 0.9 %copy-start.1 = (bf16[256,256]{1,0:T(8,128)(2,1)S(1)}, bf16[256,256]{1,0:T(8,128)(2,1)}, u32[]{:S(2)}) copy-start(bf16[256,256]{1,0:T(8,128)(2,1)} %q_hbm.1) | copy-start | bytes 393220
  2.6 0.7 %copy-start.2 = (s32[32,3]{0,1:T(4,128)S(1)}, s32[32,3]{0,1:T(4,128)}, u32[]{:S(2)}) copy-start(s32[32,3]{0,1:T(4,128)} %param.7) | copy-start | bytes 1156
